TPU v7x, 256 devices: a whole 4x4x8 slice. The times are simulated.
256 devices in a mesh: replica: 8 (over z_hi, core), fsdp: 32 (over z_lo, y, x).
Axes of the slice: x: 4, y: 4, z: 8 (z_hi: 4, z_lo: 2; z = z_hi * 2 + z_lo), core: 2. Of those that a mesh axis runs over, the one named last changes fastest.
Arguments:
- out_grad: bfloat16 [8, 16384, 8192], P('replica', 'fsdp'), may hold values from -8 to 8
- hidden_act: bfloat16 [8, 16384, 448], P('replica', 'fsdp'), may hold values from -40 to 40
- inner_params: float32 [8, 448, 8192], P('replica', None, 'fsdp'), may hold values from -6 to 6
- first_moment: float32 [8, 448, 8192], P('replica', None, 'fsdp'), may hold values from -4 to 4
- second_moment: float32 [8, 448, 8192], P('replica', None, 'fsdp'), may hold values from 0.05 to 2
- anchor: float32 [448, 8192], P(None, 'fsdp'), may hold values from -6 to 6
- outer_velocity: float32 [448, 8192], P(None, 'fsdp'), may hold values from -4 to 4
Outputs:
- new_first: float32 [8, 448, 8192], P('replica', None, 'fsdp')
- new_second: float32 [8, 448, 8192], P('replica', None, 'fsdp')
- new_anchor: float32 [448, 8192], P(None, 'fsdp')
- new_velocity: float32 [448, 8192], P(None, 'fsdp')
All inputs are finite; a program needn't handle non-finite values.
Results may differ from a plain program's by a relative error of at most 0.0003.
Values may be sent and summed in bfloat16 or wider, within the bound.
A program may use at most 128 MiB of HBM per device.

v0:
```python
import jax
import jax.numpy as jnp
from jax import lax
from jax.sharding import PartitionSpec as P

beta_one = 0.9
beta_two = 0.95
inner_rate = 0.1
decay_rate = 0.1
adam_eps = 1e-08
clip_eps = 1e-06
outer_rate = 0.7
outer_mom = 0.9
bias_one = 1.0 - 0.9**50
bias_two = 1.0 - 0.95**50


def shards(out_grad, hidden_act, inner_params, first_moment, second_moment, anchor, outer_velocity):
    cotangent = out_grad[0]
    activations = hidden_act[0]
    groups = lax.axis_size("fsdp")
    replicas = lax.axis_size("replica")
    hidden_units = activations.shape[1]
    local_columns = anchor.shape[1]
    gradient_raw = lax.psum_scatter(
        lax.dot_general(
            cotangent, activations, (((0,), (0,)), ((), ())), preferred_element_type=jnp.float32
        ),
        "fsdp",
        scatter_dimension=0,
        tiled=True,
    ).T
    squares = lax.psum(jnp.sum(gradient_raw * gradient_raw), "fsdp")
    mean_square = squares / (hidden_units * local_columns * groups)
    clip_factor = jnp.minimum(1.0, lax.rsqrt(mean_square + clip_eps))
    gradient = gradient_raw * clip_factor
    moment = beta_one * first_moment[0] + (1.0 - beta_one) * gradient
    second = beta_two * second_moment[0] + (1.0 - beta_two) * gradient * gradient
    params = inner_params[0]
    stepped = params - inner_rate * (
        moment / bias_one / (jnp.sqrt(second / bias_two) + adam_eps) + decay_rate * params
    )
    pseudo_local = anchor - stepped
    pseudo_grad = lax.psum(pseudo_local, "replica") / replicas
    velocity = outer_mom * outer_velocity + pseudo_grad
    new_anchor = anchor - outer_rate * (pseudo_grad + outer_mom * velocity)
    return (moment[None], second[None], new_anchor, velocity)


def solution(mesh):
    return jax.shard_map(
        shards,
        mesh=mesh,
        in_specs=(
            P("replica", "fsdp", None),
            P("replica", "fsdp", None),
            P("replica", None, "fsdp"),
            P("replica", None, "fsdp"),
            P("replica", None, "fsdp"),
            P(None, "fsdp"),
            P(None, "fsdp"),
        ),
        out_specs=(
            P("replica", None, "fsdp"),
            P("replica", None, "fsdp"),
            P(None, "fsdp"),
            P(None, "fsdp"),
        ),
        check_vma=False,
    )
```

profile of v0, /device:TPU:1, one launch (start us, length us, event | category | flops | bytes accessed | tf_op | source)
XLA Modules:
  0.0 383.5 jit_solution(14857170986952913494)
XLA Ops:
  7.2 0.0 copy-start
  7.2 0.0 reduce-scatter.2.cloned.1.call-start
  7.2 1.0 copy-done
  8.2 10.7 %fusion = f32[8192,448]{0,1:T(8,128)} fusion(bf16[1,512,8192]{2,1,0:T(8,128)(2,1)} %param.7, bf16[1,512,448]{1,2,0:T(8,128)(2,1)S(1)} %copy-done), kind=kOutput, calls=%fused_computation | convolution fusion | flops 3758096384 | bytes 23527424 | tf_op jit(solution)/shard_map/dot_general | solution.py:26
  18.9 0.0 copy-start.1
  18.9 0.0 copy-start.2
  18.9 0.0 copy-start.3
  18.9 0.0 copy-start.4
  18.9 0.0 copy-start.5
  18.9 0.0 reduce-scatter.2.cloned.1.call-update
  18.9 0.0 all-reduce.2.cloned.1.call-start
  19.0 183.1 %reduce-scatter.2.cloned.1.call-done = f32[256,448]{0,1:T(8,128)} async-done(((f32[8192,448]{0,1:T(8,128)}), f32[256,448]{0,1:T(8,128)}) %reduce-scatter.2.cloned.1.call-update) | async-done | bytes 458768 | tf_op jit(solution)/shard_map/reduce_scatter | solution.py:25
  202.1 1.7 multiply_reduce_fusion
  203.8 67.1 %psum.14 = f32[]{:T(128)} all-reduce(f32[]{:T(128)} %multiply_reduce_fusion), channel_id=1, replica_groups=mesh['replica'=8,'fsdp'=32] {'fsdp'}, use_global_device_ids=true, to_apply=%region_2.0 | all-reduce | flops 1 | bytes 8 | tf_op jit(solution)/shard_map/psum | solution.py:33
  271.6 0.0 copy-done.1
  271.6 0.0 copy-done.2
  271.6 0.0 copy-done.3
  271.6 0.0 copy-done.4
  271.7 2.3 fusion.5
  274.0 0.0 all-reduce.2.cloned.1.call-update
  274.0 100.6 %all-reduce.2.cloned.1.call-done = f32[448,256]{1,0:T(8,128)} async-done(((f32[448,256]{1,0:T(8,128)}), f32[448,256]{1,0:T(8,128)}) %all-reduce.2.cloned.1.call-update) | async-done | bytes 458768 | tf_op jit(solution)/shard_map/psum | solution.py:44
  374.7 0.0 copy-done.5
  374.7 2.1 multiply_subtract_fusion
Async XLA Ops:
  7.2 1.0 copy-start
  7.2 194.9 %reduce-scatter.2.cloned.1.call-start = ((), (), s32[]{:S(2)}) async-start(), calls=%async_computation.1 | async-start | bytes 15138816 | tf_op jit(solution)/shard_map/reduce_scatter | solution.py:25
  18.9 252.8 %copy-start.1 = (f32[448,256]{1,0:T(8,128)S(1)}, f32[448,256]{1,0:T(8,128)}, u32[]{:S(2)}) copy-start(f32[448,256]{1,0:T(8,128)} %param.12) | copy-start | bytes 1376260
  18.9 252.8 %copy-start.2 = (f32[1,448,256]{2,1,0:T(8,128)S(1)}, f32[1,448,256]{2,1,0:T(8,128)}, u32[]{:S(2)}) copy-start(f32[1,448,256]{2,1,0:T(8,128)} %param.9) | copy-start | bytes 1376260
  18.9 252.8 %copy-start.3 = (f32[1,448,256]{2,1,0:T(8,128)S(1)}, f32[1,448,256]{2,1,0:T(8,128)}, u32[]{:S(2)}) copy-start(f32[1,448,256]{2,1,0:T(8,128)} %param.10) | copy-start | bytes 1376260
  18.9 252.8 %copy-start.4 = (f32[1,448,256]{2,1,0:T(8,128)S(1)}, f32[1,448,256]{2,1,0:T(8,128)}, u32[]{:S(2)}) copy-start(f32[1,448,256]{2,1,0:T(8,128)} %param.11) | copy-start | bytes 1376260
  18.9 355.8 %copy-start.5 = (f32[448,256]{1,0:T(8,128)S(1)}, f32[448,256]{1,0:T(8,128)}, u32[]{:S(2)}) copy-start(f32[448,256]{1,0:T(8,128)} %param.13) | copy-start | bytes 1376260
  18.9 355.7 %all-reduce.2.cloned.1.call-start = ((), (), s32[]{:S(2)}) async-start(), calls=%async_computation.2 | async-start | bytes 917504 | tf_op jit(solution)/shard_map/psum | solution.py:44
Sparse Core Ops, SparseCore 0:
  19.0 183.0 reduce-scatter.1
  274.1 100.4 all-reduce.1
where the time goes:
time: 384 us
  waiting for transfers between devices  284 us (74%)
  blocking collectives  67.1 us (17%)
  between operations  14.8 us (4%)
  matrix products  10.7 us (3%)
  other arithmetic  6.12 us (2%)
    reduce_scatter x1, waiting for transfers between devices, shards(): lax.psum_scatter(lax.dot_general(cotangent, activations, (((0,), (0,)), (...  183 us
    psum x1, waiting for transfers between devices, shards(): pseudo_grad = lax.psum(pseudo_local, 'replica') / replicas  101 us
    psum x1, blocking collectives, shards(): squares = lax.psum(jnp.sum(gradient_raw * gradient_raw), 'fsdp')  67.1 us
    dot_general x1, matrix products, shards(): lax.dot_general(cotangent, activations, (((0,), (0,)), ((), ())), preferr...  10.7 us
  transfers between devices with their start and end apart: 2, of which 2 were waited for; matrix products, arithmetic and copies ran while one was open for 0% of the time, Pallas kernels for 0%

commit v1 on v0

v1 whole, which is shorter than its diff:
```python
import functools

import jax
import jax.numpy as jnp
from jax import lax
from jax.experimental import pallas as pl
from jax.experimental.pallas import tpu as pltpu
from jax.sharding import PartitionSpec as P

beta_one = 0.9
beta_two = 0.95
inner_rate = 0.1
decay_rate = 0.1
adam_eps = 1e-08
clip_eps = 1e-06
outer_rate = 0.7
outer_mom = 0.9
bias_one = 1.0 - 0.9**50
bias_two = 1.0 - 0.95**50

MESH = pl.DeviceIdType.MESH
LANES = 128
PAD = 16
REACH = 86.0
RING = 4
ITEMS = 8


def column_scale(values):
    largest = jnp.max(jnp.abs(values), axis=0, keepdims=True)
    return (largest * 1.01 + 1e-30).astype(jnp.bfloat16).astype(jnp.float32)


def encode(message, parts):
    rows = parts[0].shape[0]
    bounds = []
    for n, values in enumerate(parts):
        bound = column_scale(values)
        message[n * rows : (n + 1) * rows, :] = jnp.exp(values * (REACH / bound)).astype(jnp.bfloat16)
        bounds.append(bound)
    base = len(parts) * rows
    if len(parts) == 1:
        block = jnp.broadcast_to(bounds[0], (PAD, LANES))
    else:
        upper = lax.broadcasted_iota(jnp.int32, (PAD, LANES), 0) < PAD // 2
        block = jnp.where(upper, bounds[0], bounds[1])
    message[base : base + PAD, :] = block.astype(jnp.bfloat16)


def decode(message, count, which, rows):
    base = count * rows
    block = message[base : base + PAD, :].astype(jnp.float32)
    row = which * (PAD // 2) if count > 1 else 0
    bound = block[row : row + 1, :] * (1.0 / REACH)
    return jnp.log(message[which * rows : (which + 1) * rows, :].astype(jnp.float32)) * bound


def kernel(
    cotangent, activations, inner, first, second, anchor,
    gradient_out, pseudo_out,
    cot, act_t, inner_v, first_v, second_v, anchor_v,
    partial, send_a, recv_a, send_b, recv_b, send_z, recv_z,
    norm_send, norm_recv, half_send, half_recv, quarter_send, quarter_recv,
    whole_send, whole_recv, twin_recv, half_sum,
    cot_sem, state_sem, sa_sem, ra_sem, sb_sem, rb_sem, sz_sem, rz_sem,
    ns_sem, nr_sem, hs_sem, hr_sem, qs_sem, qr_sem, ws_sem, wr_sem, ts_sem, tr_sem,
):
    hidden, tokens = act_t.shape
    rows = hidden // 2
    width = 2 * LANES
    me = lax.axis_index("fsdp")
    rep = lax.axis_index("replica")
    x = me % RING
    y = (me // RING) % RING
    z = me // (RING * RING)
    core = rep % 2
    zh = rep // 2

    def at(px, py, pz):
        return {"fsdp": pz * (RING * RING) + py * RING + px}

    def twin(pzh, pcore):
        return {"replica": pzh * 2 + pcore}

    def along(axis, step):
        if axis == 0:
            return at((x + step) % RING, y, z)
        return at(x, (y + step) % RING, z)

    here = (x, y)
    pair = at(x, y, 1 - z)
    peers = [along(axis, step) for axis in (0, 1) for step in (1, 2, 3)] + [pair]
    twins = [twin((zh + step) % RING, core) for step in (1, 2, 3)]
    mate = twin(zh, 1 - core)

    halves = cotangent.shape[1] // 2
    loads = []
    for k in range(2):
        zz = (1 - z) if k == 0 else z
        loads.append(pltpu.make_async_copy(
            cotangent.at[:, pl.ds(pl.multiple_of(zz * halves, halves), halves)], cot.at[k], cot_sem.at[k]))
        loads[k].start()
    states = []
    for n, (src, dst) in enumerate(((inner, inner_v), (first, first_v), (second, second_v), (anchor, anchor_v))):
        states.append(pltpu.make_async_copy(src, dst, state_sem.at[n]))
        states[n].start()

    barrier = pltpu.get_barrier_semaphore()
    everyone = peers + twins + [mate]
    for device in everyone:
        pl.semaphore_signal(barrier, inc=1, device_id=device, device_id_type=MESH)

    act_t[...] = activations[...].T
    loads[0].wait()
    pl.semaphore_wait(barrier, len(everyone))

    def copy_a(s, axis, i, way):
        return pltpu.make_async_remote_copy(
            src_ref=send_a.at[s, i, way], dst_ref=recv_a.at[s, i, way],
            send_sem=sa_sem.at[s, i, way], recv_sem=ra_sem.at[s, i, way],
            device_id=along(axis, 1 if way == 0 else 3), device_id_type=MESH)

    def copy_b(s, axis, i, way):
        return pltpu.make_async_remote_copy(
            src_ref=send_b.at[s, i, way], dst_ref=recv_b.at[s, i, way],
            send_sem=sb_sem.at[s, i, way], recv_sem=rb_sem.at[s, i, way],
            device_id=along(axis, 1 if way == 0 else 3), device_id_type=MESH)

    def copy_z(s):
        return pltpu.make_async_remote_copy(
            src_ref=send_z.at[s], dst_ref=recv_z.at[s], send_sem=sz_sem.at[s], recv_sem=rz_sem.at[s],
            device_id=pair, device_id_type=MESH)

    def product(s, i, t):
        k, w = i // RING, i % RING
        chunk = w * RING + t if s == 0 else t * RING + w
        columns = pl.ds(pl.multiple_of(chunk * width, width), width)
        return jnp.dot(act_t[s * rows : (s + 1) * rows, :], cot[k, :, columns], preferred_element_type=jnp.float32)

    def round_a(s, axis, i, own):
        opposite = own(s, i, (here[axis] + 2) % RING)
        encode(send_a.at[s, i, 0], [opposite[:, :LANES]])
        copy_a(s, axis, i, 0).start()
        encode(send_a.at[s, i, 1], [opposite[:, LANES:]])
        copy_a(s, axis, i, 1).start()

    def round_b(s, axis, i, own):
        for way in range(2):
            value = own(s, i, (here[axis] + (1 if way == 0 else 3)) % RING)
            copy_a(s, axis, i, way).wait_recv()
            arrived = decode(recv_a.at[s, i, way], 1, 0, rows)
            left, right = value[:, :LANES], value[:, LANES:]
            if way == 0:
                left = left + arrived
            else:
                right = right + arrived
            encode(send_b.at[s, i, way], [left, right])
            copy_b(s, axis, i, way).start()

    def round_c(s, axis, i, own):
        value = own(s, i, here[axis])
        for way in range(2):
            copy_b(s, axis, i, way).wait_recv()
        parts = []
        for n in range(2):
            parts.append(value[:, n * LANES : (n + 1) * LANES]
                         + decode(recv_b.at[s, i, 0], 2, n, rows) + decode(recv_b.at[s, i, 1], 2, n, rows))
        for way in range(2):
            copy_a(s, axis, i, way).wait_send()
            copy_b(s, axis, i, way).wait_send()
        return parts

    def summed(s, i, t):
        return partial[s, i - ITEMS, t]

    def finish_other(s):
        parts = round_c(s, 1 - s, ITEMS, summed)
        encode(send_z.at[s], parts)
        copy_z(s).start()

    @pl.loop(0, ITEMS + 2)
    def _(step):
        @pl.when(step == RING)
        def _():
            pltpu.make_async_copy(
                cotangent.at[:, pl.ds(pl.multiple_of(z * halves, halves), halves)], cot.at[1], cot_sem.at[1]).wait()

        @pl.when(step < ITEMS)
        def _():
            for s in range(2):
                round_a(s, s, step, product)

        @pl.when(jnp.logical_and(step >= 1, step < ITEMS + 1))
        def _():
            for s in range(2):
                round_b(s, s, step - 1, product)

        @pl.when(step >= 2)
        def _():
            i = step - 2
            for s in range(2):
                parts = round_c(s, s, i, product)
                for n in range(2):
                    partial[s, i // RING, i % RING, :, n * LANES : (n + 1) * LANES] = parts[n]

        @pl.when(step == RING + 2)
        def _():
            for s in range(2):
                round_a(s, 1 - s, ITEMS, summed)

        @pl.when(step == RING + 3)
        def _():
            for s in range(2):
                round_b(s, 1 - s, ITEMS, summed)

        @pl.when(step == RING + 4)
        def _():
            for s in range(2):
                finish_other(s)

    last = ITEMS + 1
    for s in range(2):
        round_a(s, 1 - s, last, summed)
    for s in range(2):
        round_b(s, 1 - s, last, summed)
    total = jnp.zeros((8, LANES), jnp.float32)
    for s in range(2):
        parts = round_c(s, 1 - s, last, summed)
        copy_z(s).wait_recv()
        for n in range(2):
            value = parts[n] + decode(recv_z.at[s], 2, n, rows)
            gradient_out[s * rows : (s + 1) * rows, n * LANES : (n + 1) * LANES] = value
            total = total + jnp.sum((value * value).reshape(rows // 8, 8, LANES), axis=0)
    for s in range(2):
        copy_z(s).wait_send()

    slot = 0
    for phase in range(3):
        group = peers[3 * phase : 3 * phase + 3]
        norm_send[phase] = total
        copies = [
            pltpu.make_async_remote_copy(
                src_ref=norm_send.at[phase], dst_ref=norm_recv.at[slot + n],
                send_sem=ns_sem.at[slot + n], recv_sem=nr_sem.at[slot + n],
                device_id=device, device_id_type=MESH)
            for n, device in enumerate(group)
        ]
        for copy in copies:
            copy.start()
        if phase == 0:
            for state in states:
                state.wait()
        for copy in copies:
            copy.wait()
        for n in range(len(group)):
            total = total + norm_recv[slot + n]
        slot += len(group)

    mean_square = jnp.sum(total) / (hidden * cotangent.shape[1])
    clip_factor = jnp.minimum(1.0, lax.rsqrt(jnp.full((1, LANES), mean_square + clip_eps, jnp.float32)))

    def difference(columns):
        gradient = gradient_out[:, columns] * clip_factor
        gradient_out[:, columns] = gradient
        moment = beta_one * first_v[:, columns] + (1.0 - beta_one) * gradient
        square = beta_two * second_v[:, columns] + (1.0 - beta_two) * gradient * gradient
        params = inner_v[:, columns]
        stepped = params - inner_rate * (
            moment / bias_one / (jnp.sqrt(square / bias_two) + adam_eps) + decay_rate * params)
        return anchor_v[:, columns] - stepped

    given = pl.ds(pl.multiple_of((1 - core) * LANES, LANES), LANES)
    kept = pl.ds(pl.multiple_of(core * LANES, LANES), LANES)
    encode(half_send, [difference(given)])
    to_mate = pltpu.make_async_remote_copy(
        src_ref=half_send, dst_ref=half_recv, send_sem=hs_sem, recv_sem=hr_sem, device_id=mate, device_id_type=MESH)
    to_mate.start()
    half_sum[...] = difference(kept)
    to_mate.wait()
    half_sum[...] = half_sum[...] + decode(half_recv, 1, 0, hidden)

    piece = hidden // RING
    def rows_of(q):
        return pl.ds(pl.multiple_of(q * piece, piece), piece)

    copies = []
    for n in range(3):
        encode(quarter_send.at[n], [half_sum[rows_of((zh + n + 1) % RING), :]])
        copies.append(pltpu.make_async_remote_copy(
            src_ref=quarter_send.at[n], dst_ref=quarter_recv.at[n], send_sem=qs_sem.at[n], recv_sem=qr_sem.at[n],
            device_id=twins[n], device_id_type=MESH))
        copies[n].start()
    for copy in copies:
        copy.wait()
    mine = half_sum[rows_of(zh), :]
    for n in range(3):
        mine = mine + decode(quarter_recv.at[n], 1, 0, piece)

    encode(whole_send, [mine])
    spread = []
    for n in range(3):
        spread.append(pltpu.make_async_remote_copy(
            src_ref=whole_send, dst_ref=whole_recv.at[n], send_sem=ws_sem.at[n], recv_sem=wr_sem.at[n],
            device_id=twins[n], device_id_type=MESH))
        spread[n].start()

    def forward(source, n):
        return pltpu.make_async_remote_copy(
            src_ref=source, dst_ref=twin_recv.at[n], send_sem=ts_sem.at[n], recv_sem=tr_sem.at[n],
            device_id=mate, device_id_type=MESH)

    passed = [forward(whole_send, 3)]
    passed[0].start()
    pseudo_out[rows_of(zh), kept] = decode(whole_send, 1, 0, piece)
    for n in range(3):
        spread[n].wait_recv()
        passed.append(forward(whole_recv.at[n], n))
        passed[-1].start()
        pseudo_out[rows_of((zh + 3 - n) % RING), kept] = decode(whole_recv.at[n], 1, 0, piece)
    passed[0].wait_recv()
    pseudo_out[rows_of(zh), given] = decode(twin_recv.at[3], 1, 0, piece)
    for n in range(3):
        passed[n + 1].wait_recv()
        pseudo_out[rows_of((zh + 3 - n) % RING), given] = decode(twin_recv.at[n], 1, 0, piece)
    for copy in spread + passed:
        copy.wait_send()


def shards(out_grad, hidden_act, inner_params, first_moment, second_moment, anchor, outer_velocity):
    cotangent, activations = out_grad[0], hidden_act[0]
    tokens, hidden = activations.shape
    columns = anchor.shape[1]
    replicas = lax.axis_size("replica")
    rows = hidden // 2
    piece = hidden // RING
    bf16, f32 = jnp.bfloat16, jnp.float32
    vmem, dma = pltpu.VMEM, pltpu.SemaphoreType.DMA
    count = ITEMS + 2
    anywhere = pl.BlockSpec(memory_space=pl.ANY)
    local = pl.BlockSpec(memory_space=pltpu.VMEM)
    gradient, pseudo = pl.pallas_call(
        kernel,
        out_shape=(jax.ShapeDtypeStruct((hidden, columns), f32),) * 2,
        in_specs=[anywhere, local] + [anywhere] * 4,
        out_specs=(local, local),
        scratch_shapes=[
            vmem((2, tokens, cotangent.shape[1] // 2), bf16),
            vmem((hidden, tokens), bf16),
            *[vmem((hidden, columns), f32)] * 4,
            vmem((2, 2, RING, rows, columns), f32),
            vmem((2, count, 2, rows + PAD, LANES), bf16),
            vmem((2, count, 2, rows + PAD, LANES), bf16),
            vmem((2, count, 2, 2 * rows + PAD, LANES), bf16),
            vmem((2, count, 2, 2 * rows + PAD, LANES), bf16),
            vmem((2, 2 * rows + PAD, LANES), bf16),
            vmem((2, 2 * rows + PAD, LANES), bf16),
            vmem((3, 8, LANES), f32),
            vmem((7, 8, LANES), f32),
            vmem((hidden + PAD, LANES), bf16),
            vmem((hidden + PAD, LANES), bf16),
            vmem((3, piece + PAD, LANES), bf16),
            vmem((3, piece + PAD, LANES), bf16),
            vmem((piece + PAD, LANES), bf16),
            vmem((3, piece + PAD, LANES), bf16),
            vmem((4, piece + PAD, LANES), bf16),
            vmem((hidden, LANES), f32),
            dma((2,)), dma((4,)),
            dma((2, count, 2)), dma((2, count, 2)), dma((2, count, 2)), dma((2, count, 2)),
            dma((2,)), dma((2,)), dma((7,)), dma((7,)), dma, dma,
            dma((3,)), dma((3,)), dma((3,)), dma((3,)), dma((4,)), dma((4,)),
        ],
        compiler_params=pltpu.CompilerParams(
            collective_id=0, has_side_effects=True, vmem_limit_bytes=52 * 1024 * 1024),
        cost_estimate=pl.CostEstimate(
            flops=2 * tokens * hidden * cotangent.shape[1], bytes_accessed=12_000_000, transcendentals=8_000_000),
    )(cotangent, activations, inner_params[0], first_moment[0], second_moment[0], anchor)

    moment = beta_one * first_moment[0] + (1.0 - beta_one) * gradient
    second = beta_two * second_moment[0] + (1.0 - beta_two) * gradient * gradient
    pseudo_grad = pseudo / replicas
    velocity = outer_mom * outer_velocity + pseudo_grad
    new_anchor = anchor - outer_rate * (pseudo_grad + outer_mom * velocity)
    return (moment[None], second[None], new_anchor, velocity)


def solution(mesh):
    return jax.shard_map(
        shards,
        mesh=mesh,
        in_specs=(
            P("replica", "fsdp", None),
            P("replica", "fsdp", None),
            P("replica", None, "fsdp"),
            P("replica", None, "fsdp"),
            P("replica", None, "fsdp"),
            P(None, "fsdp"),
            P(None, "fsdp"),
        ),
        out_specs=(
            P("replica", None, "fsdp"),
            P("replica", None, "fsdp"),
            P(None, "fsdp"),
            P(None, "fsdp"),
        ),
        check_vma=False,
    )
```

time: 384 us -> 93.7 us (0.24)
  waiting for transfers between devices: 284 us -> 0 us
  Pallas kernels: 0 us -> 86.6 us
  blocking collectives: 67.1 us -> 0 us
  between operations: 14.8 us -> 0.66 us
  matrix products: 10.7 us -> 0 us
  other arithmetic: 6.12 us -> 2.09 us
    reduce_scatter x1 -> x0, waiting for transfers between devices: 183 us -> none  [shards(): lax.psum_scatter(lax.dot_general(cotangent, activations, (((0,), (0,)), (...]
    psum x1 -> x0, waiting for transfers between devices: 101 us -> none  [shards(): pseudo_grad = lax.psum(pseudo_local, 'replica') / replicas]
    pallas_call x0 -> x1, Pallas kernels: none -> 86.6 us  [shards(): pl.pallas_call(kernel, out_shape=(jax.ShapeDtypeStruct((hidden, columns),...]
    psum x1 -> x0, blocking collectives: 67.1 us -> none  [shards(): squares = lax.psum(jnp.sum(gradient_raw * gradient_raw), 'fsdp')]
    dot_general x1 -> x0, matrix products: 10.7 us -> none  [shards(): lax.dot_general(cotangent, activations, (((0,), (0,)), ((), ())), preferr...]
  transfers between devices with their start and end apart: 2 -> 0, of which waited for: 2 -> 0; matrix products, arithmetic and copies ran while one was open for 0% -> 0% of each run, Pallas kernels for 0% -> 0%
where the time goes in v1:
time: 93.7 us; the launch traced here: 93.5 us
  Pallas kernels  86.6 us (92%)
  local copies, waits for them, and re-layouts  4.12 us (4%)
  other arithmetic  2.09 us (2%)
    pallas_call x1, Pallas kernels, shards(): pl.pallas_call(kernel, out_shape=(jax.ShapeDtypeStruct((hidden, columns),...  86.6 us
    unnamed x11, local copies, waits for them, and re-layouts  4.12 us

profile of v1, /device:TPU:1, one launch (start us, length us, event | category | flops | bytes accessed | tf_op | source)
XLA Modules:
  0.0 93.5 jit_solution(2238641770526065317)
XLA Ops:
  0.6 0.0 copy-start.2
  0.6 2.1 %copy.11 = bf16[1,512,448]{2,1,0:T(8,128)(2,1)} copy(bf16[1,512,448]{1,2,0:T(8,128)(2,1)} %param.8) | data formatting | bytes 917504 | tf_op args[1]
  2.7 0.0 copy-start
  2.7 1.0 %copy-done = f32[1,448,256]{2,1,0:T(8,128)S(1)} copy-done((f32[1,448,256]{2,1,0:T(8,128)S(1)}, f32[1,448,256]{2,1,0:T(8,128)}, u32[]{:S(2)}) %copy-start) | copy-done | bytes 458776
  3.7 0.0 copy-start.1
  3.7 1.0 %copy-done.1 = f32[1,448,256]{2,1,0:T(8,128)S(1)} copy-done((f32[1,448,256]{2,1,0:T(8,128)S(1)}, f32[1,448,256]{2,1,0:T(8,128)}, u32[]{:S(2)}) %copy-start.1) | copy-done | bytes 458776
  4.7 0.0 copy-start.3
  4.8 0.0 copy-start.4
  4.8 86.6 %shard_map.102 = (f32[448,256]{1,0:T(8,128)S(1)}, f32[448,256]{1,0:T(8,128)S(1)}) custom-call(bf16[512,8192]{1,0:T(8,128)(2,1)} %bitcast.15, bf16[512,448]{1,0:T(8,128)(2,1)} %bitcast.13, f32[448,256]{1,0:T(8,128)S(1)} %bitcast.12, f32[448,256]{1,0:T(8,128)S(1)} %bitcast.11, f32[448,256]{1,0:T(8,128)} %bitcast.14, f32[448,256]{1,0:T(8,128)} %anchor.1), custom_call_target="tpu_custom_call" | custom-call | flops 3758096384 | bytes 12000000 | tf_op jit(solution)/shard_map/pallas_call | solution.py:341
  91.4 0.0 copy-done.2
  91.4 1.1 %fusion.1 = (f32[1,448,256]{2,1,0:T(8,128)}, f32[1,448,256]{2,1,0:T(8,128)}) fusion(f32[448,256]{1,0:T(8,128)S(1)} %get-tuple-element.6, f32[1,448,256]{2,1,0:T(8,128)S(1)} %copy-done.2, f32[1,448,256]{2,1,0:T(8,128)S(1)} %copy-done), kind=kLoop, calls=%fused_computation.2 | loop fusion | flops 802816 | bytes 2293760 | tf_op jit(solution)/shard_map/broadcast_in_dim | solution.py:383
  92.5 0.0 copy-done.3
  92.5 0.0 copy-done.4
  92.5 1.0 %multiply_subtract_fusion = (f32[448,256]{1,0:T(8,128)}, f32[448,256]{1,0:T(8,128)}) fusion(f32[448,256]{1,0:T(8,128)S(1)} %copy-done.3, f32[448,256]{1,0:T(8,128)S(1)} %get-tuple-element.7, f32[448,256]{1,0:T(8,128)S(1)} %copy-done.4), kind=kLoop, calls=%fused_computation.3 | loop fusion | flops 802816 | bytes 2293760 | tf_op jit(solution)/shard_map/sub | solution.py:382
Async XLA Ops:
  0.6 90.8 %copy-start.2 = (f32[1,448,256]{2,1,0:T(8,128)S(1)}, f32[1,448,256]{2,1,0:T(8,128)}, u32[]{:S(2)}) copy-start(f32[1,448,256]{2,1,0:T(8,128)} %param.11) | copy-start | bytes 1376260
  2.7 1.0 %copy-start = (f32[1,448,256]{2,1,0:T(8,128)S(1)}, f32[1,448,256]{2,1,0:T(8,128)}, u32[]{:S(2)}) copy-start(f32[1,448,256]{2,1,0:T(8,128)} %param.10) | copy-start | bytes 1376260
  3.7 1.0 %copy-start.1 = (f32[1,448,256]{2,1,0:T(8,128)S(1)}, f32[1,448,256]{2,1,0:T(8,128)}, u32[]{:S(2)}) copy-start(f32[1,448,256]{2,1,0:T(8,128)} %param.9) | copy-start | bytes 1376260
  4.7 87.7 %copy-start.3 = (f32[448,256]{1,0:T(8,128)S(1)}, f32[448,256]{1,0:T(8,128)}, u32[]{:S(2)}) copy-start(f32[448,256]{1,0:T(8,128)} %anchor.1) | copy-start | bytes 1376260
  4.8 87.7 %copy-start.4 = (f32[448,256]{1,0:T(8,128)S(1)}, f32[448,256]{1,0:T(8,128)}, u32[]{:S(2)}) copy-start(f32[448,256]{1,0:T(8,128)} %param.13) | copy-start | bytes 1376260

commit v2 on v1

v2 whole, which is shorter than its diff:
```python
import functools

import jax
import jax.numpy as jnp
from jax import lax
from jax.experimental import pallas as pl
from jax.experimental.pallas import tpu as pltpu
from jax.sharding import PartitionSpec as P

beta_one = 0.9
beta_two = 0.95
inner_rate = 0.1
decay_rate = 0.1
adam_eps = 1e-08
clip_eps = 1e-06
outer_rate = 0.7
outer_mom = 0.9
bias_one = 1.0 - 0.9**50
bias_two = 1.0 - 0.95**50

MESH = pl.DeviceIdType.MESH
LANES = 128
PAD = 16
REACH = 86.0
RING = 4
ITEMS = 8


def column_scale(values):
    largest = jnp.max(jnp.abs(values), axis=0, keepdims=True)
    return (largest * 1.01 + 1e-30).astype(jnp.bfloat16).astype(jnp.float32)


def encode(message, parts):
    rows = parts[0].shape[0]
    bounds = []
    for n, values in enumerate(parts):
        bound = column_scale(values)
        message[n * rows : (n + 1) * rows, :] = jnp.exp(values * (REACH / bound)).astype(jnp.bfloat16)
        bounds.append(bound)
    base = len(parts) * rows
    if len(parts) == 1:
        block = jnp.broadcast_to(bounds[0], (PAD, LANES))
    else:
        upper = lax.broadcasted_iota(jnp.int32, (PAD, LANES), 0) < PAD // 2
        block = jnp.where(upper, bounds[0], bounds[1])
    message[base : base + PAD, :] = block.astype(jnp.bfloat16)


def decode(message, count, which, rows):
    base = count * rows
    block = message[base : base + PAD, :].astype(jnp.float32)
    row = which * (PAD // 2) if count > 1 else 0
    bound = block[row : row + 1, :] * (1.0 / REACH)
    return jnp.log(message[which * rows : (which + 1) * rows, :].astype(jnp.float32)) * bound


def kernel(
    cotangent, act_t, inner, first, second, anchor, velocity,
    first_out, second_out, anchor_out, velocity_out,
    cot, inner_v, first_v, second_v, anchor_v, velocity_v,
    partial, send_a, recv_a, send_b, recv_b, send_z, recv_z,
    norm_send, norm_recv, half_send, half_recv, swap_send, swap_recv, pseudo,
    cot_sem, state_sem, sa_sem, ra_sem, sb_sem, rb_sem, sz_sem, rz_sem,
    ns_sem, nr_sem, hs_sem, hr_sem, ws_sem, wr_sem, ts_sem, tr_sem,
):
    hidden, tokens = act_t.shape
    rows = hidden // 2
    width = 2 * LANES
    me = lax.axis_index("fsdp")
    rep = lax.axis_index("replica")
    x = me % RING
    y = (me // RING) % RING
    z = me // (RING * RING)
    core = rep % 2
    zh = rep // 2

    def at(px, py, pz):
        return {"fsdp": pz * (RING * RING) + py * RING + px}

    def twin(pzh, pcore):
        return {"replica": pzh * 2 + pcore}

    def along(axis, step):
        if axis == 0:
            return at((x + step) % RING, y, z)
        return at(x, (y + step) % RING, z)

    here = (x, y)
    pair = at(x, y, 1 - z)
    mate = twin(zh, 1 - core)
    partners = (twin(zh + 1 - 2 * (zh % 2), core), twin(RING - 1 - zh, core))
    norm_groups = (
        [along(0, step) for step in (1, 2, 3)],
        [along(1, step) for step in (1, 2, 3)] + [at(x, (y + step) % RING, 1 - z) for step in range(RING)],
    )

    halves = cotangent.shape[1] // 2

    def load(k):
        zz = (1 - z) if k == 0 else z
        return pltpu.make_async_copy(
            cotangent.at[:, pl.ds(pl.multiple_of(zz * halves, halves), halves)], cot.at[k], cot_sem.at[k])

    load(0).start()
    load(1).start()
    states = []
    for n, (src, dst) in enumerate((
        (inner, inner_v), (first, first_v), (second, second_v), (anchor, anchor_v), (velocity, velocity_v),
    )):
        states.append(pltpu.make_async_copy(src, dst, state_sem.at[n]))
        states[n].start()

    barrier = pltpu.get_barrier_semaphore()
    everyone = norm_groups[0] + norm_groups[1] + [mate, *partners]
    for device in everyone:
        pl.semaphore_signal(barrier, inc=1, device_id=device, device_id_type=MESH)
    load(0).wait()
    pl.semaphore_wait(barrier, len(everyone))

    def copy_a(s, axis, i, way):
        return pltpu.make_async_remote_copy(
            src_ref=send_a.at[s, i, way], dst_ref=recv_a.at[s, i, way],
            send_sem=sa_sem.at[s, i, way], recv_sem=ra_sem.at[s, i, way],
            device_id=along(axis, 1 if way == 0 else 3), device_id_type=MESH)

    def copy_b(s, axis, i, way):
        return pltpu.make_async_remote_copy(
            src_ref=send_b.at[s, i, way], dst_ref=recv_b.at[s, i, way],
            send_sem=sb_sem.at[s, i, way], recv_sem=rb_sem.at[s, i, way],
            device_id=along(axis, 1 if way == 0 else 3), device_id_type=MESH)

    def copy_z(s):
        return pltpu.make_async_remote_copy(
            src_ref=send_z.at[s], dst_ref=recv_z.at[s], send_sem=sz_sem.at[s], recv_sem=rz_sem.at[s],
            device_id=pair, device_id_type=MESH)

    def offset(i):
        j = i % RING
        return jnp.where(j == 0, 2, jnp.where(j == 1, 1, jnp.where(j == 2, 3, 0)))

    def product(s, i, t):
        w = (here[1 - s] + offset(i)) % RING
        chunk = w * RING + t if s == 0 else t * RING + w
        columns = pl.ds(pl.multiple_of(chunk * width, width), width)
        return jnp.dot(act_t[s * rows : (s + 1) * rows, :], cot[i // RING, :, columns], preferred_element_type=jnp.float32)

    def round_a(s, axis, i, own):
        opposite = own(s, i, (here[axis] + 2) % RING)
        encode(send_a.at[s, i, 0], [opposite[:, :LANES]])
        copy_a(s, axis, i, 0).start()
        encode(send_a.at[s, i, 1], [opposite[:, LANES:]])
        copy_a(s, axis, i, 1).start()

    def round_b(s, axis, i, own):
        for way in range(2):
            value = own(s, i, (here[axis] + (1 if way == 0 else 3)) % RING)
            copy_a(s, axis, i, way).wait_recv()
            arrived = decode(recv_a.at[s, i, way], 1, 0, rows)
            left, right = value[:, :LANES], value[:, LANES:]
            if way == 0:
                left = left + arrived
            else:
                right = right + arrived
            encode(send_b.at[s, i, way], [left, right])
            copy_b(s, axis, i, way).start()

    def round_c(s, axis, i, own):
        value = own(s, i, here[axis])
        for way in range(2):
            copy_b(s, axis, i, way).wait_recv()
        parts = []
        for n in range(2):
            parts.append(value[:, n * LANES : (n + 1) * LANES]
                         + decode(recv_b.at[s, i, 0], 2, n, rows) + decode(recv_b.at[s, i, 1], 2, n, rows))
        for way in range(2):
            copy_a(s, axis, i, way).wait_send()
            copy_b(s, axis, i, way).wait_send()
        return parts

    def summed(s, i, t):
        return partial[s, i - ITEMS, t]

    @pl.loop(0, ITEMS + 2)
    def _(step):
        @pl.when(step == RING)
        def _():
            load(1).wait()

        @pl.when(step < ITEMS)
        def _():
            for s in range(2):
                round_a(s, s, step, product)

        @pl.when(jnp.logical_and(step >= 1, step < ITEMS + 1))
        def _():
            for s in range(2):
                round_b(s, s, step - 1, product)

        @pl.when(step >= 2)
        def _():
            i = step - 2
            for s in range(2):
                parts = round_c(s, s, i, product)
                w = (here[1 - s] + offset(i)) % RING
                for n in range(2):
                    partial[s, i // RING, w, :, n * LANES : (n + 1) * LANES] = parts[n]

        later = ITEMS + (step - 2) // RING

        @pl.when(jnp.logical_or(step == 2, step == RING + 2))
        def _():
            for s in range(2):
                round_a(s, 1 - s, later, summed)

        @pl.when(jnp.logical_or(step == 4, step == RING + 4))
        def _():
            for s in range(2):
                round_b(s, 1 - s, later, summed)

        @pl.when(step == RING + 2)
        def _():
            for s in range(2):
                encode(send_z.at[s], round_c(s, 1 - s, ITEMS, summed))
                copy_z(s).start()

    for state in states:
        state.wait()
    last = ITEMS + 1
    total = jnp.zeros((8, LANES), jnp.float32)
    for s in range(2):
        copy_z(s).wait_recv()
        parts = round_c(s, 1 - s, last, summed)
        for n in range(2):
            value = parts[n] + decode(recv_z.at[s], 2, n, rows)
            first_out[s * rows : (s + 1) * rows, n * LANES : (n + 1) * LANES] = value
            total = total + jnp.sum((value * value).reshape(rows // 8, 8, LANES), axis=0)

    slot = 0
    sent = []
    for phase, group in enumerate(norm_groups):
        norm_send[phase] = total
        copies = [
            pltpu.make_async_remote_copy(
                src_ref=norm_send.at[phase], dst_ref=norm_recv.at[slot + n],
                send_sem=ns_sem.at[slot + n], recv_sem=nr_sem.at[slot + n],
                device_id=device, device_id_type=MESH)
            for n, device in enumerate(group)
        ]
        for copy in copies:
            copy.start()
        for n, copy in enumerate(copies):
            copy.wait_recv()
            total = total + norm_recv[slot + n]
        slot += len(group)
        sent += copies

    mean_square = jnp.sum(total) / (hidden * cotangent.shape[1])
    clip_factor = jnp.minimum(1.0, lax.rsqrt(jnp.full((1, LANES), mean_square + clip_eps, jnp.float32)))

    def difference(part, columns):
        gradient = first_out[part, columns] * clip_factor
        moment = beta_one * first_v[part, columns] + (1.0 - beta_one) * gradient
        square = beta_two * second_v[part, columns] + (1.0 - beta_two) * gradient * gradient
        first_out[part, columns] = moment
        second_out[part, columns] = square
        params = inner_v[part, columns]
        stepped = params - inner_rate * (
            moment / bias_one / (jnp.sqrt(square / bias_two) + adam_eps) + decay_rate * params)
        return anchor_v[part, columns] - stepped

    given = pl.ds(pl.multiple_of((1 - core) * LANES, LANES), LANES)
    kept = pl.ds(pl.multiple_of(core * LANES, LANES), LANES)
    parts = [slice(0, rows), slice(rows, hidden)]

    def to_mate(n):
        return pltpu.make_async_remote_copy(
            src_ref=half_send.at[n], dst_ref=half_recv.at[n], send_sem=hs_sem.at[n], recv_sem=hr_sem.at[n],
            device_id=mate, device_id_type=MESH)

    def swap(n, turn):
        return pltpu.make_async_remote_copy(
            src_ref=swap_send.at[n, turn], dst_ref=swap_recv.at[n, turn],
            send_sem=ws_sem.at[n, turn], recv_sem=wr_sem.at[n, turn],
            device_id=partners[(n + turn) % 2], device_id_type=MESH)

    def share(n):
        block = pseudo.at[core, n]
        return pltpu.make_async_remote_copy(
            src_ref=block, dst_ref=block, send_sem=ts_sem.at[n], recv_sem=tr_sem.at[n],
            device_id=mate, device_id_type=MESH)

    for n in range(2):
        half_send[n] = difference(parts[n], given)
        to_mate(n).start()
    mine = [difference(parts[n], kept) for n in range(2)]
    for n in range(2):
        to_mate(n).wait_recv()
        encode(swap_send.at[n, 0], [mine[n] + half_recv[n]])
        swap(n, 0).start()
    for n in range(2):
        own = decode(swap_send.at[n, 0], 1, 0, rows)
        swap(n, 0).wait_recv()
        encode(swap_send.at[n, 1], [own + decode(swap_recv.at[n, 0], 1, 0, rows)])
        swap(n, 1).start()

    def finish(n, which, columns):
        pseudo_grad = pseudo[which, n] / (2 * RING)
        moved = outer_mom * velocity_v[parts[n], columns] + pseudo_grad
        velocity_out[parts[n], columns] = moved
        anchor_out[parts[n], columns] = anchor_v[parts[n], columns] - outer_rate * (pseudo_grad + outer_mom * moved)

    for n in range(2):
        own = decode(swap_send.at[n, 1], 1, 0, rows)
        swap(n, 1).wait_recv()
        pseudo[core, n] = own + decode(swap_recv.at[n, 1], 1, 0, rows)
        share(n).start()
    for n in range(2):
        finish(n, core, kept)
    for copy in sent + [copy_z(0), copy_z(1), to_mate(0), to_mate(1)]:
        copy.wait_send()
    for n in range(2):
        for turn in range(2):
            swap(n, turn).wait_send()
    for n in range(2):
        share(n).wait_recv()
        finish(n, 1 - core, given)
    for n in range(2):
        share(n).wait_send()


def shards(out_grad, hidden_act, inner_params, first_moment, second_moment, anchor, outer_velocity):
    cotangent, act_t = out_grad[0], hidden_act[0].T
    hidden, tokens = act_t.shape
    columns = anchor.shape[1]
    rows = hidden // 2
    bf16, f32 = jnp.bfloat16, jnp.float32
    vmem, dma = pltpu.VMEM, pltpu.SemaphoreType.DMA
    count = ITEMS + 2
    anywhere = pl.BlockSpec(memory_space=pltpu.HBM)
    local = pl.BlockSpec(memory_space=pltpu.VMEM)
    moment, second, new_anchor, new_velocity = pl.pallas_call(
        kernel,
        out_shape=(jax.ShapeDtypeStruct((hidden, columns), f32),) * 4,
        in_specs=[anywhere, local] + [anywhere] * 5,
        out_specs=(local,) * 4,
        scratch_shapes=[
            vmem((2, tokens, cotangent.shape[1] // 2), bf16),
            *[vmem((hidden, columns), f32)] * 5,
            vmem((2, 2, RING, rows, columns), f32),
            vmem((2, count, 2, rows + PAD, LANES), bf16),
            vmem((2, count, 2, rows + PAD, LANES), bf16),
            vmem((2, count, 2, 2 * rows + PAD, LANES), bf16),
            vmem((2, count, 2, 2 * rows + PAD, LANES), bf16),
            vmem((2, 2 * rows + PAD, LANES), bf16),
            vmem((2, 2 * rows + PAD, LANES), bf16),
            vmem((2, 8, LANES), f32),
            vmem((10, 8, LANES), f32),
            vmem((2, rows, LANES), f32),
            vmem((2, rows, LANES), f32),
            vmem((2, 2, rows + PAD, LANES), bf16),
            vmem((2, 2, rows + PAD, LANES), bf16),
            vmem((2, 2, rows, LANES), f32),
            dma((2,)), dma((5,)),
            dma((2, count, 2)), dma((2, count, 2)), dma((2, count, 2)), dma((2, count, 2)),
            dma((2,)), dma((2,)), dma((10,)), dma((10,)), dma((2,)), dma((2,)),
            dma((2, 2)), dma((2, 2)), dma((2,)), dma((2,)),
        ],
        compiler_params=pltpu.CompilerParams(
            collective_id=0, has_side_effects=True, vmem_limit_bytes=52 * 1024 * 1024),
        cost_estimate=pl.CostEstimate(
            flops=2 * tokens * hidden * cotangent.shape[1], bytes_accessed=12_000_000, transcendentals=8_000_000),
    )(cotangent, act_t, inner_params[0], first_moment[0], second_moment[0], anchor, outer_velocity)
    return (moment[None], second[None], new_anchor, new_velocity)


def solution(mesh):
    return jax.shard_map(
        shards,
        mesh=mesh,
        in_specs=(
            P("replica", "fsdp", None),
            P("replica", "fsdp", None),
            P("replica", None, "fsdp"),
            P("replica", None, "fsdp"),
            P("replica", None, "fsdp"),
            P(None, "fsdp"),
            P(None, "fsdp"),
        ),
        out_specs=(
            P("replica", None, "fsdp"),
            P("replica", None, "fsdp"),
            P(None, "fsdp"),
            P(None, "fsdp"),
        ),
        check_vma=False,
    )
```

time: 93.7 us -> 81.2 us (0.87)
  Pallas kernels: 86.6 us -> 77.3 us
  other arithmetic: 2.09 us -> 0 us
  local copies, waits for them, and re-layouts: 4.12 us -> 3.07 us
    pallas_call x1, Pallas kernels: 86.6 us -> 77.3 us  [shards(): pl.pallas_call(kernel, out_shape=(jax.ShapeDtypeStruct((hidden, columns),...]
    broadcast_in_dim x1 -> x0, other arithmetic: 1.06 us -> none  [shards(): return (moment[None], second[None], new_anchor, velocity)]
    unnamed x11 -> x4, local copies, waits for them, and re-layouts: 4.12 us -> 3.07 us
    sub x1 -> x0, other arithmetic: 1.04 us -> none  [shards(): new_anchor = anchor - outer_rate * (pseudo_grad + outer_mom * velocity)]
where the time goes in v2:
time: 81.2 us; the launch traced here: 81.1 us
  Pallas kernels  77.3 us (95%)
  local copies, waits for them, and re-layouts  3.07 us (4%)
    pallas_call x1, Pallas kernels, shards(): pl.pallas_call(kernel, out_shape=(jax.ShapeDtypeStruct((hidden, columns),...  77.3 us
    unnamed x4, local copies, waits for them, and re-layouts  3.07 us

profile of v2, /device:TPU:1, one launch (start us, length us, event | category | flops | bytes accessed | tf_op | source)
XLA Modules:
  0.0 81.1 jit_solution(11493185553329630549)
XLA Ops:
  0.6 77.3 %shard_map.102 = (f32[448,256]{1,0:T(8,128)S(1)}, f32[448,256]{1,0:T(8,128)S(1)}, f32[448,256]{1,0:T(8,128)S(1)}, f32[448,256]{1,0:T(8,128)S(1)}) custom-call(bf16[512,8192]{1,0:T(8,128)(2,1)} %bitcast.11, bf16[448,512]{1,0:T(8,128)(2,1)} %bitcast.12, f32[448,256]{1,0:T(8,128)} %bitcast.13, f32[448,256]{1,0:T(8,128)} %bitcast.14, f32[448,256]{1,0:T(8,128)} %bitcast.15, ...), custom_call_target="tpu_custom_call" | custom-call | flops 3758096384 | bytes 12000000 | tf_op jit(solution)/shard_map/pallas_call | solution.py:342
  78.0 0.8 copy.15
  78.8 0.8 copy.16
  79.5 0.8 copy.17
  80.3 0.8 copy.18

commit v3 on v2

--- a/solution.py
+++ b/solution.py
@@ -24,6 +24,22 @@
 REACH = 86.0
 RING = 4
 ITEMS = 8
+SPANS = ((0, 128), (128, 192), (320, 128))
+COUNTS = (ITEMS + 2, ITEMS + 2, RING + 1)
+ROUND_A, ROUND_B, ROUND_C, EARLY, CROSS = range(5)
+SCHEDULE = (
+    (0, 0, 0), (0, 1, 0), (3, 2, 2), (0, 0, 4), (0, 1, 1), (0, 0, 6), (0, 1, 6), (0, 0, 2),
+    (0, 0, 1), (3, 2, 0), (0, 0, 3), (0, 0, 5), (3, 2, 1), (0, 1, 3), (1, 0, 0), (0, 1, 2),
+    (3, 2, 4), (0, 1, 4), (1, 1, 0), (1, 0, 4), (3, 2, 6), (1, 0, 2), (1, 0, 6), (1, 1, 1),
+    (3, 2, 3), (0, 2, 0), (0, 2, 1), (0, 0, 7), (1, 1, 2), (1, 1, 4), (0, 1, 5), (2, 1, 0),
+    (0, 1, 8), (1, 0, 1), (2, 0, 4), (1, 2, 0), (1, 1, 3), (0, 2, 2), (2, 1, 1), (2, 0, 6),
+    (1, 0, 5), (3, 2, 5), (1, 1, 6), (2, 0, 0), (2, 0, 2), (0, 0, 8), (2, 1, 2), (1, 1, 8),
+    (1, 2, 1), (0, 1, 7), (2, 0, 1), (2, 2, 0), (0, 2, 3), (3, 2, 7), (1, 1, 5), (1, 2, 2),
+    (2, 1, 4), (0, 2, 4), (0, 1, 9), (1, 0, 3), (0, 0, 9), (1, 0, 8), (2, 1, 3), (1, 1, 7),
+    (1, 0, 7), (2, 1, 6), (1, 2, 3), (2, 2, 1), (2, 0, 5), (2, 2, 2), (4, 1, 8), (1, 2, 4),
+    (1, 0, 9), (2, 1, 5), (1, 1, 9), (2, 0, 3), (4, 0, 8), (2, 2, 3), (2, 2, 4), (2, 1, 7),
+    (2, 0, 7), (2, 0, 9), (2, 1, 9),
+)
 
 
 def column_scale(values):
@@ -39,18 +55,18 @@
         message[n * rows : (n + 1) * rows, :] = jnp.exp(values * (REACH / bound)).astype(jnp.bfloat16)
         bounds.append(bound)
     base = len(parts) * rows
-    if len(parts) == 1:
-        block = jnp.broadcast_to(bounds[0], (PAD, LANES))
-    else:
-        upper = lax.broadcasted_iota(jnp.int32, (PAD, LANES), 0) < PAD // 2
-        block = jnp.where(upper, bounds[0], bounds[1])
+    share = PAD // len(parts)
+    line = lax.broadcasted_iota(jnp.int32, (PAD, LANES), 0)
+    block = jnp.broadcast_to(bounds[-1], (PAD, LANES))
+    for n in range(len(parts) - 2, -1, -1):
+        block = jnp.where(line < (n + 1) * share, bounds[n], block)
     message[base : base + PAD, :] = block.astype(jnp.bfloat16)
 
 
 def decode(message, count, which, rows):
     base = count * rows
     block = message[base : base + PAD, :].astype(jnp.float32)
-    row = which * (PAD // 2) if count > 1 else 0
+    row = which * (PAD // count)
     bound = block[row : row + 1, :] * (1.0 / REACH)
     return jnp.log(message[which * rows : (which + 1) * rows, :].astype(jnp.float32)) * bound
 
@@ -59,14 +75,20 @@
     cotangent, act_t, inner, first, second, anchor, velocity,
     first_out, second_out, anchor_out, velocity_out,
     cot, inner_v, first_v, second_v, anchor_v, velocity_v,
-    partial, send_a, recv_a, send_b, recv_b, send_z, recv_z,
+    partial, other_partial, third_partial,
+    send_a0, send_a1, send_a2, recv_a0, recv_a1, recv_a2, send_b0, send_b1, send_b2, recv_b0, recv_b1, recv_b2,
+    send_z0, send_z1, recv_z0, recv_z1, send_early, recv_early,
     norm_send, norm_recv, half_send, half_recv, swap_send, swap_recv, pseudo,
-    cot_sem, state_sem, sa_sem, ra_sem, sb_sem, rb_sem, sz_sem, rz_sem,
+    cot_sem, state_sem, sa_sem, ra_sem, sb_sem, rb_sem, sz_sem, rz_sem, se_sem, re_sem,
     ns_sem, nr_sem, hs_sem, hr_sem, ws_sem, wr_sem, ts_sem, tr_sem,
 ):
     hidden, tokens = act_t.shape
-    rows = hidden // 2
+    half = hidden // 2
     width = 2 * LANES
+    sums = (partial, other_partial, third_partial)
+    send_a, recv_a = (send_a0, send_a1, send_a2), (recv_a0, recv_a1, recv_a2)
+    send_b, recv_b = (send_b0, send_b1, send_b2), (recv_b0, recv_b1, recv_b2)
+    send_z, recv_z = (send_z0, send_z1), (recv_z0, recv_z1)
     me = lax.axis_index("fsdp")
     rep = lax.axis_index("replica")
     x = me % RING
@@ -115,126 +137,151 @@
     everyone = norm_groups[0] + norm_groups[1] + [mate, *partners]
     for device in everyone:
         pl.semaphore_signal(barrier, inc=1, device_id=device, device_id_type=MESH)
-    load(0).wait()
-    pl.semaphore_wait(barrier, len(everyone))
-
     def copy_a(s, axis, i, way):
         return pltpu.make_async_remote_copy(
-            src_ref=send_a.at[s, i, way], dst_ref=recv_a.at[s, i, way],
+            src_ref=send_a[s].at[i, way], dst_ref=recv_a[s].at[i, way],
             send_sem=sa_sem.at[s, i, way], recv_sem=ra_sem.at[s, i, way],
             device_id=along(axis, 1 if way == 0 else 3), device_id_type=MESH)
 
     def copy_b(s, axis, i, way):
         return pltpu.make_async_remote_copy(
-            src_ref=send_b.at[s, i, way], dst_ref=recv_b.at[s, i, way],
+            src_ref=send_b[s].at[i, way], dst_ref=recv_b[s].at[i, way],
             send_sem=sb_sem.at[s, i, way], recv_sem=rb_sem.at[s, i, way],
             device_id=along(axis, 1 if way == 0 else 3), device_id_type=MESH)
 
     def copy_z(s):
         return pltpu.make_async_remote_copy(
-            src_ref=send_z.at[s], dst_ref=recv_z.at[s], send_sem=sz_sem.at[s], recv_sem=rz_sem.at[s],
+            src_ref=send_z[s], dst_ref=recv_z[s], send_sem=sz_sem.at[s], recv_sem=rz_sem.at[s],
             device_id=pair, device_id_type=MESH)
 
+    def copy_early(j):
+        return pltpu.make_async_remote_copy(
+            src_ref=send_early.at[j], dst_ref=recv_early.at[j], send_sem=se_sem.at[j], recv_sem=re_sem.at[j],
+            device_id=pair, device_id_type=MESH)
+
     def offset(i):
-        j = i % RING
-        return jnp.where(j == 0, 2, jnp.where(j == 1, 1, jnp.where(j == 2, 3, 0)))
-
-    def product(s, i, t):
+        return (2, 1, 3, 0)[i % RING]
+
+    def dot(s, k, chunk):
+        columns = pl.ds(pl.multiple_of(chunk * width, width), width)
+        first_row, rows = SPANS[s]
+        return jnp.dot(act_t[first_row : first_row + rows, :], cot[k, :, columns], preferred_element_type=jnp.float32)
+
+    def product(s, i, step):
         w = (here[1 - s] + offset(i)) % RING
-        chunk = w * RING + t if s == 0 else t * RING + w
-        columns = pl.ds(pl.multiple_of(chunk * width, width), width)
-        return jnp.dot(act_t[s * rows : (s + 1) * rows, :], cot[i // RING, :, columns], preferred_element_type=jnp.float32)
+        t = (here[s] + step) % RING
+        return dot(s, i // RING, w * RING + t if s == 0 else t * RING + w)
+
+    def paired(s, n, step):
+        order = (2, 1, 3, 0).index(step)
+        w = (y + offset(n)) % RING
+        t = (x + step) % RING
+        j = 2 * n + order // 2
+        if order in (0, 2):
+            copy_early(j).wait_recv()
+        _, rows = SPANS[s]
+        arrived = recv_early.at[j]
+        both = [decode(arrived, 4, 2 * (order % 2) + h, rows) for h in range(2)]
+        return dot(s, 1, w * RING + t) + jnp.concatenate(both, axis=1)
+
+    def summed(s, i, step):
+        axis = 1 if s != 1 else 0
+        k = i - ITEMS if s < 2 else 0
+        return sums[s][k, (here[axis] + step) % RING]
+
+    def fill_a(s, axis, i, own):
+        opposite = own(s, i, 2)
+        encode(send_a[s].at[i, 0], [opposite[:, :LANES]])
+        encode(send_a[s].at[i, 1], [opposite[:, LANES:]])
+
+    def start_a(s, axis, i):
+        for way in range(2):
+            copy_a(s, axis, i, way).start()
 
     def round_a(s, axis, i, own):
-        opposite = own(s, i, (here[axis] + 2) % RING)
-        encode(send_a.at[s, i, 0], [opposite[:, :LANES]])
-        copy_a(s, axis, i, 0).start()
-        encode(send_a.at[s, i, 1], [opposite[:, LANES:]])
-        copy_a(s, axis, i, 1).start()
+        fill_a(s, axis, i, own)
+        start_a(s, axis, i)
 
     def round_b(s, axis, i, own):
+        _, rows = SPANS[s]
         for way in range(2):
-            value = own(s, i, (here[axis] + (1 if way == 0 else 3)) % RING)
+            value = own(s, i, 1 if way == 0 else 3)
             copy_a(s, axis, i, way).wait_recv()
-            arrived = decode(recv_a.at[s, i, way], 1, 0, rows)
+            arrived = decode(recv_a[s].at[i, way], 1, 0, rows)
             left, right = value[:, :LANES], value[:, LANES:]
             if way == 0:
                 left = left + arrived
             else:
                 right = right + arrived
-            encode(send_b.at[s, i, way], [left, right])
+            encode(send_b[s].at[i, way], [left, right])
             copy_b(s, axis, i, way).start()
 
     def round_c(s, axis, i, own):
-        value = own(s, i, here[axis])
+        _, rows = SPANS[s]
+        value = own(s, i, 0)
         for way in range(2):
             copy_b(s, axis, i, way).wait_recv()
         parts = []
         for n in range(2):
             parts.append(value[:, n * LANES : (n + 1) * LANES]
-                         + decode(recv_b.at[s, i, 0], 2, n, rows) + decode(recv_b.at[s, i, 1], 2, n, rows))
+                         + decode(recv_b[s].at[i, 0], 2, n, rows) + decode(recv_b[s].at[i, 1], 2, n, rows))
         for way in range(2):
             copy_a(s, axis, i, way).wait_send()
             copy_b(s, axis, i, way).wait_send()
         return parts
 
-    def summed(s, i, t):
-        return partial[s, i - ITEMS, t]
-
-    @pl.loop(0, ITEMS + 2)
-    def _(step):
-        @pl.when(step == RING)
-        def _():
+    def keep(s, k, w, parts):
+        for n in range(2):
+            sums[s][k, w, :, n * LANES : (n + 1) * LANES] = parts[n]
+
+    def send_pair(j):
+        w = (y + offset(j // 2)) % RING
+        parts = []
+        for step in ((2, 1), (3, 0))[j % 2]:
+            value = dot(2, 0, w * RING + (x + step) % RING)
+            parts += [value[:, :LANES], value[:, LANES:]]
+        encode(send_early.at[j], parts)
+        copy_early(j).start()
+
+    total = jnp.zeros((8, LANES), jnp.float32)
+    loaded = False
+    load(0).wait()
+    for s in range(2):
+        fill_a(s, s, 0, product)
+    pl.semaphore_wait(barrier, len(everyone))
+    for s in range(2):
+        start_a(s, s, 0)
+    for task, s, i in SCHEDULE[2:]:
+        later = i >= COUNTS[s] - (2 if s < 2 else 1)
+        axis = (1 if s == 0 else 0) if later and s < 2 else (1 if later or s == 1 else 0)
+        own = summed if later else (product if s < 2 else paired)
+        if not loaded and not later and task in (ROUND_A, ROUND_B, ROUND_C) and (s == 2 or i >= RING):
             load(1).wait()
-
-        @pl.when(step < ITEMS)
-        def _():
-            for s in range(2):
-                round_a(s, s, step, product)
-
-        @pl.when(jnp.logical_and(step >= 1, step < ITEMS + 1))
-        def _():
-            for s in range(2):
-                round_b(s, s, step - 1, product)
-
-        @pl.when(step >= 2)
-        def _():
-            i = step - 2
-            for s in range(2):
-                parts = round_c(s, s, i, product)
-                w = (here[1 - s] + offset(i)) % RING
-                for n in range(2):
-                    partial[s, i // RING, w, :, n * LANES : (n + 1) * LANES] = parts[n]
-
-        later = ITEMS + (step - 2) // RING
-
-        @pl.when(jnp.logical_or(step == 2, step == RING + 2))
-        def _():
-            for s in range(2):
-                round_a(s, 1 - s, later, summed)
-
-        @pl.when(jnp.logical_or(step == 4, step == RING + 4))
-        def _():
-            for s in range(2):
-                round_b(s, 1 - s, later, summed)
-
-        @pl.when(step == RING + 2)
-        def _():
-            for s in range(2):
-                encode(send_z.at[s], round_c(s, 1 - s, ITEMS, summed))
-                copy_z(s).start()
-
+            loaded = True
+        if task == EARLY:
+            send_pair(i)
+        elif task == CROSS:
+            encode(send_z[s], round_c(s, 1 - s, ITEMS, summed))
+            copy_z(s).start()
+        elif task == ROUND_A:
+            round_a(s, axis, i, own)
+        elif task == ROUND_B:
+            round_b(s, axis, i, own)
+        elif not later:
+            keep(s, i // RING, ((here[1 - s] if s < 2 else y) + offset(i)) % RING, round_c(s, axis, i, own))
+        elif i == COUNTS[s] - 1:
+            first_row, rows = SPANS[s]
+            parts = round_c(s, axis, i, own)
+            if s < 2:
+                copy_z(s).wait_recv()
+            for n in range(2):
+                value = parts[n]
+                if s < 2:
+                    value = value + decode(recv_z[s], 2, n, rows)
+                first_out[first_row : first_row + rows, n * LANES : (n + 1) * LANES] = value
+                total = total + jnp.sum((value * value).reshape(rows // 8, 8, LANES), axis=0)
     for state in states:
         state.wait()
-    last = ITEMS + 1
-    total = jnp.zeros((8, LANES), jnp.float32)
-    for s in range(2):
-        copy_z(s).wait_recv()
-        parts = round_c(s, 1 - s, last, summed)
-        for n in range(2):
-            value = parts[n] + decode(recv_z.at[s], 2, n, rows)
-            first_out[s * rows : (s + 1) * rows, n * LANES : (n + 1) * LANES] = value
-            total = total + jnp.sum((value * value).reshape(rows // 8, 8, LANES), axis=0)
 
     slot = 0
     sent = []
@@ -271,7 +318,7 @@
 
     given = pl.ds(pl.multiple_of((1 - core) * LANES, LANES), LANES)
     kept = pl.ds(pl.multiple_of(core * LANES, LANES), LANES)
-    parts = [slice(0, rows), slice(rows, hidden)]
+    parts = [slice(0, half), slice(half, hidden)]
 
     def to_mate(n):
         return pltpu.make_async_remote_copy(
@@ -299,9 +346,9 @@
         encode(swap_send.at[n, 0], [mine[n] + half_recv[n]])
         swap(n, 0).start()
     for n in range(2):
-        own = decode(swap_send.at[n, 0], 1, 0, rows)
+        own = decode(swap_send.at[n, 0], 1, 0, half)
         swap(n, 0).wait_recv()
-        encode(swap_send.at[n, 1], [own + decode(swap_recv.at[n, 0], 1, 0, rows)])
+        encode(swap_send.at[n, 1], [own + decode(swap_recv.at[n, 0], 1, 0, half)])
         swap(n, 1).start()
 
     def finish(n, which, columns):
@@ -311,13 +358,13 @@
         anchor_out[parts[n], columns] = anchor_v[parts[n], columns] - outer_rate * (pseudo_grad + outer_mom * moved)
 
     for n in range(2):
-        own = decode(swap_send.at[n, 1], 1, 0, rows)
+        own = decode(swap_send.at[n, 1], 1, 0, half)
         swap(n, 1).wait_recv()
-        pseudo[core, n] = own + decode(swap_recv.at[n, 1], 1, 0, rows)
+        pseudo[core, n] = own + decode(swap_recv.at[n, 1], 1, 0, half)
         share(n).start()
     for n in range(2):
         finish(n, core, kept)
-    for copy in sent + [copy_z(0), copy_z(1), to_mate(0), to_mate(1)]:
+    for copy in sent + [copy_z(0), copy_z(1), to_mate(0), to_mate(1)] + [copy_early(j) for j in range(ITEMS)]:
         copy.wait_send()
     for n in range(2):
         for turn in range(2):
@@ -327,13 +374,23 @@
         finish(n, 1 - core, given)
     for n in range(2):
         share(n).wait_send()
+
+
+def place(*refs):
+    count = len(refs) // 2
+    sems = refs[-1]
+    copies = [pltpu.make_async_copy(refs[n], refs[count + n], sems.at[n]) for n in range(count)]
+    for copy in copies:
+        copy.start()
+    for copy in copies:
+        copy.wait()
 
 
 def shards(out_grad, hidden_act, inner_params, first_moment, second_moment, anchor, outer_velocity):
     cotangent, act_t = out_grad[0], hidden_act[0].T
     hidden, tokens = act_t.shape
     columns = anchor.shape[1]
-    rows = hidden // 2
+    half = hidden // 2
     bf16, f32 = jnp.bfloat16, jnp.float32
     vmem, dma = pltpu.VMEM, pltpu.SemaphoreType.DMA
     count = ITEMS + 2
@@ -347,23 +404,21 @@
         scratch_shapes=[
             vmem((2, tokens, cotangent.shape[1] // 2), bf16),
             *[vmem((hidden, columns), f32)] * 5,
-            vmem((2, 2, RING, rows, columns), f32),
-            vmem((2, count, 2, rows + PAD, LANES), bf16),
-            vmem((2, count, 2, rows + PAD, LANES), bf16),
-            vmem((2, count, 2, 2 * rows + PAD, LANES), bf16),
-            vmem((2, count, 2, 2 * rows + PAD, LANES), bf16),
-            vmem((2, 2 * rows + PAD, LANES), bf16),
-            vmem((2, 2 * rows + PAD, LANES), bf16),
+            *[vmem((2 if s < 2 else 1, RING, rows, columns), f32) for s, (_, rows) in enumerate(SPANS)],
+            *[vmem((count, 2, rows + PAD, LANES), bf16) for count, (_, rows) in zip(COUNTS, SPANS)] * 2,
+            *[vmem((count, 2, 2 * rows + PAD, LANES), bf16) for count, (_, rows) in zip(COUNTS, SPANS)] * 2,
+            *[vmem((2 * rows + PAD, LANES), bf16) for _, rows in SPANS[:2]] * 2,
+            *[vmem((ITEMS, 4 * SPANS[2][1] + PAD, LANES), bf16)] * 2,
             vmem((2, 8, LANES), f32),
             vmem((10, 8, LANES), f32),
-            vmem((2, rows, LANES), f32),
-            vmem((2, rows, LANES), f32),
-            vmem((2, 2, rows + PAD, LANES), bf16),
-            vmem((2, 2, rows + PAD, LANES), bf16),
-            vmem((2, 2, rows, LANES), f32),
+            vmem((2, half, LANES), f32),
+            vmem((2, half, LANES), f32),
+            vmem((2, 2, half + PAD, LANES), bf16),
+            vmem((2, 2, half + PAD, LANES), bf16),
+            vmem((2, 2, half, LANES), f32),
             dma((2,)), dma((5,)),
-            dma((2, count, 2)), dma((2, count, 2)), dma((2, count, 2)), dma((2, count, 2)),
-            dma((2,)), dma((2,)), dma((10,)), dma((10,)), dma((2,)), dma((2,)),
+            *[dma((3, count, 2))] * 4,
+            dma((2,)), dma((2,)), dma((ITEMS,)), dma((ITEMS,)), dma((10,)), dma((10,)), dma((2,)), dma((2,)),
             dma((2, 2)), dma((2, 2)), dma((2,)), dma((2,)),
         ],
         compiler_params=pltpu.CompilerParams(
@@ -371,6 +426,15 @@
         cost_estimate=pl.CostEstimate(
             flops=2 * tokens * hidden * cotangent.shape[1], bytes_accessed=12_000_000, transcendentals=8_000_000),
     )(cotangent, act_t, inner_params[0], first_moment[0], second_moment[0], anchor, outer_velocity)
+    moment, second, new_anchor, new_velocity = pl.pallas_call(
+        place,
+        out_shape=(jax.ShapeDtypeStruct((hidden, columns), f32),) * 4,
+        in_specs=[local] * 4,
+        out_specs=(anywhere,) * 4,
+        scratch_shapes=[dma((4,))],
+        compiler_params=pltpu.CompilerParams(vmem_limit_bytes=4 * 1024 * 1024),
+        cost_estimate=pl.CostEstimate(flops=0, bytes_accessed=32 * hidden * columns, transcendentals=0),
+    )(moment, second, new_anchor, new_velocity)
     return (moment[None], second[None], new_anchor, new_velocity)
 
 

time: 81.2 us -> 74.1 us (0.913)
  Pallas kernels: 77.3 us -> 73.2 us
  local copies, waits for them, and re-layouts: 3.07 us -> 0 us
    pallas_call x1, Pallas kernels: 77.3 us -> 71.9 us  [shards(): pl.pallas_call(kernel, out_shape=(jax.ShapeDtypeStruct((hidden, columns),...]
    unnamed x4 -> x0, local copies, waits for them, and re-layouts: 3.07 us -> none
    pallas_call x0 -> x1, Pallas kernels: none -> 1.26 us  [shards(): pl.pallas_call(place, out_shape=(jax.ShapeDtypeStruct((hidden, columns),...]
where the time goes in v3:
time: 74.1 us; the launch traced here: 74 us
  Pallas kernels  73.2 us (99%)
  between operations  0.8 us (1%)
    pallas_call x1, Pallas kernels, shards(): pl.pallas_call(kernel, out_shape=(jax.ShapeDtypeStruct((hidden, columns),...  71.9 us

profile of v3, /device:TPU:1, one launch (start us, length us, event | category | flops | bytes accessed | tf_op | source)
XLA Modules:
  0.0 74.0 jit_solution(4933881329502321482)
XLA Ops:
  0.6 71.9 %shard_map.102 = (f32[448,256]{1,0:T(8,128)S(1)}, f32[448,256]{1,0:T(8,128)S(1)}, f32[448,256]{1,0:T(8,128)S(1)}, f32[448,256]{1,0:T(8,128)S(1)}) custom-call(bf16[512,8192]{1,0:T(8,128)(2,1)} %bitcast.9, bf16[448,512]{1,0:T(8,128)(2,1)} %bitcast.10, f32[448,256]{1,0:T(8,128)} %bitcast.11, f32[448,256]{1,0:T(8,128)} %bitcast.12, f32[448,256]{1,0:T(8,128)} %bitcast.13, ...), custom_call_target="tpu_custom_call" | custom-call | flops 3758096384 | bytes 12000000 | tf_op jit(solution)/shard_map/pallas_call | solution.py:399
  72.5 1.3 %shard_map.103 = (f32[448,256]{1,0:T(8,128)}, f32[448,256]{1,0:T(8,128)}, f32[448,256]{1,0:T(8,128)}, f32[448,256]{1,0:T(8,128)}) custom-call(f32[448,256]{1,0:T(8,128)S(1)} %get-tuple-element.12.refs_0_, f32[448,256]{1,0:T(8,128)S(1)} %get-tuple-element.13.refs_1_, f32[448,256]{1,0:T(8,128)S(1)} %get-tuple-element.14.refs_2_, ...), custom_call_target="tpu_custom_call" | custom-call | bytes 3670016 | tf_op jit(solution)/shard_map/pallas_call | solution.py:429

commit v4 on v3

--- a/solution.py
+++ b/solution.py
@@ -24,21 +24,21 @@
 REACH = 86.0
 RING = 4
 ITEMS = 8
-SPANS = ((0, 128), (128, 192), (320, 128))
+BLOCKS = (128, 192, 144)
 COUNTS = (ITEMS + 2, ITEMS + 2, RING + 1)
 ROUND_A, ROUND_B, ROUND_C, EARLY, CROSS = range(5)
 SCHEDULE = (
-    (0, 0, 0), (0, 1, 0), (3, 2, 2), (0, 0, 4), (0, 1, 1), (0, 0, 6), (0, 1, 6), (0, 0, 2),
-    (0, 0, 1), (3, 2, 0), (0, 0, 3), (0, 0, 5), (3, 2, 1), (0, 1, 3), (1, 0, 0), (0, 1, 2),
-    (3, 2, 4), (0, 1, 4), (1, 1, 0), (1, 0, 4), (3, 2, 6), (1, 0, 2), (1, 0, 6), (1, 1, 1),
-    (3, 2, 3), (0, 2, 0), (0, 2, 1), (0, 0, 7), (1, 1, 2), (1, 1, 4), (0, 1, 5), (2, 1, 0),
-    (0, 1, 8), (1, 0, 1), (2, 0, 4), (1, 2, 0), (1, 1, 3), (0, 2, 2), (2, 1, 1), (2, 0, 6),
-    (1, 0, 5), (3, 2, 5), (1, 1, 6), (2, 0, 0), (2, 0, 2), (0, 0, 8), (2, 1, 2), (1, 1, 8),
-    (1, 2, 1), (0, 1, 7), (2, 0, 1), (2, 2, 0), (0, 2, 3), (3, 2, 7), (1, 1, 5), (1, 2, 2),
-    (2, 1, 4), (0, 2, 4), (0, 1, 9), (1, 0, 3), (0, 0, 9), (1, 0, 8), (2, 1, 3), (1, 1, 7),
-    (1, 0, 7), (2, 1, 6), (1, 2, 3), (2, 2, 1), (2, 0, 5), (2, 2, 2), (4, 1, 8), (1, 2, 4),
-    (1, 0, 9), (2, 1, 5), (1, 1, 9), (2, 0, 3), (4, 0, 8), (2, 2, 3), (2, 2, 4), (2, 1, 7),
-    (2, 0, 7), (2, 0, 9), (2, 1, 9),
+    (0, 0, 0), (0, 1, 0), (3, 2, 0), (0, 0, 7), (0, 0, 2), (3, 2, 4), (0, 1, 4), (0, 0, 1),
+    (0, 1, 2), (0, 1, 1), (0, 0, 3), (0, 0, 4), (1, 0, 0), (0, 1, 6), (3, 2, 2), (0, 0, 5),
+    (1, 1, 0), (1, 0, 2), (0, 0, 6), (1, 0, 3), (0, 2, 0), (1, 1, 1), (1, 1, 2), (3, 2, 1),
+    (0, 1, 3), (1, 0, 4), (2, 0, 0), (2, 1, 0), (3, 2, 6), (0, 1, 8), (0, 2, 2), (0, 1, 5),
+    (3, 2, 5), (2, 0, 2), (1, 0, 5), (0, 0, 8), (1, 1, 4), (1, 0, 1), (3, 2, 3), (2, 0, 4),
+    (1, 0, 6), (2, 1, 1), (1, 1, 6), (2, 1, 2), (2, 0, 3), (1, 2, 0), (1, 1, 3), (0, 0, 9),
+    (0, 2, 1), (3, 2, 7), (1, 1, 8), (0, 2, 3), (2, 0, 1), (1, 0, 8), (2, 1, 4), (0, 1, 7),
+    (2, 0, 6), (1, 1, 5), (2, 0, 5), (2, 2, 0), (0, 1, 9), (1, 2, 2), (2, 1, 3), (0, 2, 4),
+    (1, 0, 9), (1, 2, 1), (1, 0, 7), (1, 1, 7), (1, 2, 3), (4, 1, 8), (2, 2, 2), (2, 1, 6),
+    (2, 1, 5), (1, 1, 9), (2, 2, 1), (1, 2, 4), (4, 0, 8), (2, 0, 7), (2, 0, 9), (2, 2, 3),
+    (2, 1, 7), (2, 2, 4), (2, 1, 9),
 )
 
 
@@ -47,34 +47,30 @@
     return (largest * 1.01 + 1e-30).astype(jnp.bfloat16).astype(jnp.float32)
 
 
+def last_line():
+    return lax.broadcasted_iota(jnp.int32, (PAD, LANES), 0) == PAD - 1
+
+
 def encode(message, parts):
     rows = parts[0].shape[0]
-    bounds = []
     for n, values in enumerate(parts):
         bound = column_scale(values)
-        message[n * rows : (n + 1) * rows, :] = jnp.exp(values * (REACH / bound)).astype(jnp.bfloat16)
-        bounds.append(bound)
-    base = len(parts) * rows
-    share = PAD // len(parts)
-    line = lax.broadcasted_iota(jnp.int32, (PAD, LANES), 0)
-    block = jnp.broadcast_to(bounds[-1], (PAD, LANES))
-    for n in range(len(parts) - 2, -1, -1):
-        block = jnp.where(line < (n + 1) * share, bounds[n], block)
-    message[base : base + PAD, :] = block.astype(jnp.bfloat16)
-
-
-def decode(message, count, which, rows):
-    base = count * rows
-    block = message[base : base + PAD, :].astype(jnp.float32)
-    row = which * (PAD // count)
-    bound = block[row : row + 1, :] * (1.0 / REACH)
-    return jnp.log(message[which * rows : (which + 1) * rows, :].astype(jnp.float32)) * bound
+        coded = jnp.exp(values * (REACH / bound))
+        end = (n + 1) * rows
+        message[n * rows : end - PAD, :] = coded[: rows - PAD].astype(jnp.bfloat16)
+        message[end - PAD : end, :] = jnp.where(last_line(), bound, coded[rows - PAD :]).astype(jnp.bfloat16)
+
+
+def decode(message, which, rows):
+    block = message[which * rows : (which + 1) * rows, :].astype(jnp.float32)
+    values = jnp.log(block) * (block[rows - 1 : rows, :] * (1.0 / REACH))
+    return jnp.concatenate([values[: rows - PAD], jnp.where(last_line(), 0.0, values[rows - PAD :])], axis=0)
 
 
 def kernel(
-    cotangent, act_t, inner, first, second, anchor, velocity,
+    cotangent, activations, inner, first, second, anchor, velocity,
     first_out, second_out, anchor_out, velocity_out,
-    cot, inner_v, first_v, second_v, anchor_v, velocity_v,
+    cot, act_t, inner_v, first_v, second_v, anchor_v, velocity_v,
     partial, other_partial, third_partial,
     send_a0, send_a1, send_a2, recv_a0, recv_a1, recv_a2, send_b0, send_b1, send_b2, recv_b0, recv_b1, recv_b2,
     send_z0, send_z1, recv_z0, recv_z1, send_early, recv_early,
@@ -82,8 +78,8 @@
     cot_sem, state_sem, sa_sem, ra_sem, sb_sem, rb_sem, sz_sem, rz_sem, se_sem, re_sem,
     ns_sem, nr_sem, hs_sem, hr_sem, ws_sem, wr_sem, ts_sem, tr_sem,
 ):
-    hidden, tokens = act_t.shape
-    half = hidden // 2
+    hidden, tokens = activations.shape
+    piece = hidden // RING
     width = 2 * LANES
     sums = (partial, other_partial, third_partial)
     send_a, recv_a = (send_a0, send_a1, send_a2), (recv_a0, recv_a1, recv_a2)
@@ -164,7 +160,7 @@
 
     def dot(s, k, chunk):
         columns = pl.ds(pl.multiple_of(chunk * width, width), width)
-        first_row, rows = SPANS[s]
+        first_row, rows = sum(BLOCKS[:s]), BLOCKS[s]
         return jnp.dot(act_t[first_row : first_row + rows, :], cot[k, :, columns], preferred_element_type=jnp.float32)
 
     def product(s, i, step):
@@ -179,9 +175,9 @@
         j = 2 * n + order // 2
         if order in (0, 2):
             copy_early(j).wait_recv()
-        _, rows = SPANS[s]
+        rows = BLOCKS[s]
         arrived = recv_early.at[j]
-        both = [decode(arrived, 4, 2 * (order % 2) + h, rows) for h in range(2)]
+        both = [decode(arrived, 2 * (order % 2) + h, rows) for h in range(2)]
         return dot(s, 1, w * RING + t) + jnp.concatenate(both, axis=1)
 
     def summed(s, i, step):
@@ -203,11 +199,11 @@
         start_a(s, axis, i)
 
     def round_b(s, axis, i, own):
-        _, rows = SPANS[s]
+        rows = BLOCKS[s]
         for way in range(2):
             value = own(s, i, 1 if way == 0 else 3)
             copy_a(s, axis, i, way).wait_recv()
-            arrived = decode(recv_a[s].at[i, way], 1, 0, rows)
+            arrived = decode(recv_a[s].at[i, way], 0, rows)
             left, right = value[:, :LANES], value[:, LANES:]
             if way == 0:
                 left = left + arrived
@@ -217,14 +213,14 @@
             copy_b(s, axis, i, way).start()
 
     def round_c(s, axis, i, own):
-        _, rows = SPANS[s]
+        rows = BLOCKS[s]
         value = own(s, i, 0)
         for way in range(2):
             copy_b(s, axis, i, way).wait_recv()
         parts = []
         for n in range(2):
             parts.append(value[:, n * LANES : (n + 1) * LANES]
-                         + decode(recv_b[s].at[i, 0], 2, n, rows) + decode(recv_b[s].at[i, 1], 2, n, rows))
+                         + decode(recv_b[s].at[i, 0], n, rows) + decode(recv_b[s].at[i, 1], n, rows))
         for way in range(2):
             copy_a(s, axis, i, way).wait_send()
             copy_b(s, axis, i, way).wait_send()
@@ -245,6 +241,22 @@
 
     total = jnp.zeros((8, LANES), jnp.float32)
     loaded = False
+    spares = []
+    ends = (BLOCKS[0], hidden)
+    inside = hidden - BLOCKS[0] - BLOCKS[2]
+    middle = BLOCKS[0] + inside
+    after = BLOCKS[0] + BLOCKS[1]
+    line = lax.broadcasted_iota(jnp.int32, (PAD, tokens), 0)
+    spare = jnp.zeros((PAD, tokens), jnp.float32)
+    for n, (end, place_end) in enumerate(zip(ends, (BLOCKS[0], sum(BLOCKS)))):
+        tail_rows = activations[end - PAD : end, :].astype(jnp.float32)
+        act_t[place_end - PAD : place_end, :] = jnp.where(line == PAD - 1, 0.0, tail_rows).astype(jnp.bfloat16)
+        spare = jnp.where(line == n, tail_rows[PAD - 1 : PAD, :], spare)
+    act_t[: BLOCKS[0] - PAD, :] = activations[: BLOCKS[0] - PAD, :]
+    act_t[BLOCKS[0] : middle, :] = activations[BLOCKS[0] : middle, :]
+    act_t[middle : middle + PAD, :] = spare.astype(jnp.bfloat16)
+    act_t[after : sum(BLOCKS) - PAD, :] = activations[middle : hidden - PAD, :]
+
     load(0).wait()
     for s in range(2):
         fill_a(s, s, 0, product)
@@ -270,16 +282,22 @@
         elif not later:
             keep(s, i // RING, ((here[1 - s] if s < 2 else y) + offset(i)) % RING, round_c(s, axis, i, own))
         elif i == COUNTS[s] - 1:
-            first_row, rows = SPANS[s]
+            rows = BLOCKS[s]
+            start, taken = ((0, rows), (BLOCKS[0], inside), (middle, rows))[s]
             parts = round_c(s, axis, i, own)
             if s < 2:
                 copy_z(s).wait_recv()
             for n in range(2):
                 value = parts[n]
                 if s < 2:
-                    value = value + decode(recv_z[s], 2, n, rows)
-                first_out[first_row : first_row + rows, n * LANES : (n + 1) * LANES] = value
+                    value = value + decode(recv_z[s], n, rows)
+                first_out[start : start + taken, n * LANES : (n + 1) * LANES] = value[:taken]
+                if s == 1:
+                    spares.append(value[taken : taken + 8])
                 total = total + jnp.sum((value * value).reshape(rows // 8, 8, LANES), axis=0)
+    for n in range(2):
+        for row, end in enumerate(ends):
+            first_out[end - 1 : end, n * LANES : (n + 1) * LANES] = spares[n][row : row + 1]
     for state in states:
         state.wait()
 
@@ -318,7 +336,7 @@
 
     given = pl.ds(pl.multiple_of((1 - core) * LANES, LANES), LANES)
     kept = pl.ds(pl.multiple_of(core * LANES, LANES), LANES)
-    parts = [slice(0, half), slice(half, hidden)]
+    parts = [slice(n * piece, (n + 1) * piece) for n in range(RING)]
 
     def to_mate(n):
         return pltpu.make_async_remote_copy(
@@ -337,18 +355,21 @@
             src_ref=block, dst_ref=block, send_sem=ts_sem.at[n], recv_sem=tr_sem.at[n],
             device_id=mate, device_id_type=MESH)
 
-    for n in range(2):
+    def widen(values):
+        return jnp.concatenate([values, jnp.zeros((PAD, LANES), jnp.float32)], axis=0)
+
+    for n in range(RING):
         half_send[n] = difference(parts[n], given)
         to_mate(n).start()
-    mine = [difference(parts[n], kept) for n in range(2)]
-    for n in range(2):
+    mine = [difference(parts[n], kept) for n in range(RING)]
+    for n in range(RING):
         to_mate(n).wait_recv()
-        encode(swap_send.at[n, 0], [mine[n] + half_recv[n]])
+        encode(swap_send.at[n, 0], [widen(mine[n] + half_recv[n])])
         swap(n, 0).start()
-    for n in range(2):
-        own = decode(swap_send.at[n, 0], 1, 0, half)
+    for n in range(RING):
+        own = decode(swap_send.at[n, 0], 0, piece + PAD)
         swap(n, 0).wait_recv()
-        encode(swap_send.at[n, 1], [own + decode(swap_recv.at[n, 0], 1, 0, half)])
+        encode(swap_send.at[n, 1], [own + decode(swap_recv.at[n, 0], 0, piece + PAD)])
         swap(n, 1).start()
 
     def finish(n, which, columns):
@@ -357,22 +378,22 @@
         velocity_out[parts[n], columns] = moved
         anchor_out[parts[n], columns] = anchor_v[parts[n], columns] - outer_rate * (pseudo_grad + outer_mom * moved)
 
-    for n in range(2):
-        own = decode(swap_send.at[n, 1], 1, 0, half)
+    for n in range(RING):
+        own = decode(swap_send.at[n, 1], 0, piece + PAD)
         swap(n, 1).wait_recv()
-        pseudo[core, n] = own + decode(swap_recv.at[n, 1], 1, 0, half)
+        pseudo[core, n] = (own + decode(swap_recv.at[n, 1], 0, piece + PAD))[:piece]
         share(n).start()
-    for n in range(2):
+    for n in range(RING):
         finish(n, core, kept)
-    for copy in sent + [copy_z(0), copy_z(1), to_mate(0), to_mate(1)] + [copy_early(j) for j in range(ITEMS)]:
+    for copy in sent + [copy_z(0), copy_z(1), *[to_mate(n) for n in range(RING)]] + [copy_early(j) for j in range(ITEMS)]:
         copy.wait_send()
-    for n in range(2):
+    for n in range(RING):
         for turn in range(2):
             swap(n, turn).wait_send()
-    for n in range(2):
+    for n in range(RING):
         share(n).wait_recv()
         finish(n, 1 - core, given)
-    for n in range(2):
+    for n in range(RING):
         share(n).wait_send()
 
 
@@ -390,7 +411,7 @@
     cotangent, act_t = out_grad[0], hidden_act[0].T
     hidden, tokens = act_t.shape
     columns = anchor.shape[1]
-    half = hidden // 2
+    piece = hidden // RING
     bf16, f32 = jnp.bfloat16, jnp.float32
     vmem, dma = pltpu.VMEM, pltpu.SemaphoreType.DMA
     count = ITEMS + 2
@@ -403,23 +424,24 @@
         out_specs=(local,) * 4,
         scratch_shapes=[
             vmem((2, tokens, cotangent.shape[1] // 2), bf16),
+            vmem((sum(BLOCKS), tokens), bf16),
             *[vmem((hidden, columns), f32)] * 5,
-            *[vmem((2 if s < 2 else 1, RING, rows, columns), f32) for s, (_, rows) in enumerate(SPANS)],
-            *[vmem((count, 2, rows + PAD, LANES), bf16) for count, (_, rows) in zip(COUNTS, SPANS)] * 2,
-            *[vmem((count, 2, 2 * rows + PAD, LANES), bf16) for count, (_, rows) in zip(COUNTS, SPANS)] * 2,
-            *[vmem((2 * rows + PAD, LANES), bf16) for _, rows in SPANS[:2]] * 2,
-            *[vmem((ITEMS, 4 * SPANS[2][1] + PAD, LANES), bf16)] * 2,
+            *[vmem((2 if s < 2 else 1, RING, rows, columns), f32) for s, rows in enumerate(BLOCKS)],
+            *[vmem((count, 2, rows, LANES), bf16) for count, rows in zip(COUNTS, BLOCKS)] * 2,
+            *[vmem((count, 2, 2 * rows, LANES), bf16) for count, rows in zip(COUNTS, BLOCKS)] * 2,
+            *[vmem((2 * rows, LANES), bf16) for rows in BLOCKS[:2]] * 2,
+            *[vmem((ITEMS, 4 * BLOCKS[2], LANES), bf16)] * 2,
             vmem((2, 8, LANES), f32),
             vmem((10, 8, LANES), f32),
-            vmem((2, half, LANES), f32),
-            vmem((2, half, LANES), f32),
-            vmem((2, 2, half + PAD, LANES), bf16),
-            vmem((2, 2, half + PAD, LANES), bf16),
-            vmem((2, 2, half, LANES), f32),
+            vmem((RING, piece, LANES), f32),
+            vmem((RING, piece, LANES), f32),
+            vmem((RING, 2, piece + PAD, LANES), bf16),
+            vmem((RING, 2, piece + PAD, LANES), bf16),
+            vmem((2, RING, piece, LANES), f32),
             dma((2,)), dma((5,)),
             *[dma((3, count, 2))] * 4,
-            dma((2,)), dma((2,)), dma((ITEMS,)), dma((ITEMS,)), dma((10,)), dma((10,)), dma((2,)), dma((2,)),
-            dma((2, 2)), dma((2, 2)), dma((2,)), dma((2,)),
+            dma((2,)), dma((2,)), dma((ITEMS,)), dma((ITEMS,)), dma((10,)), dma((10,)), dma((RING,)), dma((RING,)),
+            dma((RING, 2)), dma((RING, 2)), dma((RING,)), dma((RING,)),
         ],
         compiler_params=pltpu.CompilerParams(
             collective_id=0, has_side_effects=True, vmem_limit_bytes=52 * 1024 * 1024),

time: 74.1 us -> 72.2 us (0.974)
  Pallas kernels: 73.2 us -> 71.3 us
    pallas_call x1, Pallas kernels: 71.9 us -> 70 us  [shards(): pl.pallas_call(kernel, out_shape=(jax.ShapeDtypeStruct((hidden, columns),...]
where the time goes in v4:
time: 72.2 us; the launch traced here: 72.1 us
  Pallas kernels  71.3 us (99%)
  between operations  0.8 us (1%)
    pallas_call x1, Pallas kernels, shards(): pl.pallas_call(kernel, out_shape=(jax.ShapeDtypeStruct((hidden, columns),...  70 us

profile of v4, /device:TPU:1, one launch (start us, length us, event | category | flops | bytes accessed | tf_op | source)
XLA Modules:
  0.0 72.1 jit_solution(267821418963441187)
XLA Ops:
  0.6 70.0 %shard_map.102 = (f32[448,256]{1,0:T(8,128)S(1)}, f32[448,256]{1,0:T(8,128)S(1)}, f32[448,256]{1,0:T(8,128)S(1)}, f32[448,256]{1,0:T(8,128)S(1)}) custom-call(bf16[512,8192]{1,0:T(8,128)(2,1)} %bitcast.9, bf16[448,512]{1,0:T(8,128)(2,1)} %bitcast.10, f32[448,256]{1,0:T(8,128)} %bitcast.11, f32[448,256]{1,0:T(8,128)} %bitcast.12, f32[448,256]{1,0:T(8,128)} %bitcast.13, ...), custom_call_target="tpu_custom_call" | custom-call | flops 3758096384 | bytes 12000000 | tf_op jit(solution)/shard_map/pallas_call | solution.py:420
  70.7 1.3 %shard_map.103 = (f32[448,256]{1,0:T(8,128)}, f32[448,256]{1,0:T(8,128)}, f32[448,256]{1,0:T(8,128)}, f32[448,256]{1,0:T(8,128)}) custom-call(f32[448,256]{1,0:T(8,128)S(1)} %get-tuple-element.12.refs_0_, f32[448,256]{1,0:T(8,128)S(1)} %get-tuple-element.13.refs_1_, f32[448,256]{1,0:T(8,128)S(1)} %get-tuple-element.14.refs_2_, ...), custom_call_target="tpu_custom_call" | custom-call | bytes 3670016 | tf_op jit(solution)/shard_map/pallas_call | solution.py:451

commit v5 on v4

--- a/solution.py
+++ b/solution.py
@@ -1,4 +1,4 @@
-import functools
+import itertools
 
 import jax
 import jax.numpy as jnp
@@ -23,6 +23,7 @@
 PAD = 16
 REACH = 86.0
 RING = 4
+GROUP = 2 * RING * RING
 ITEMS = 8
 BLOCKS = (128, 192, 144)
 COUNTS = (ITEMS + 2, ITEMS + 2, RING + 1)
@@ -108,10 +109,13 @@
     pair = at(x, y, 1 - z)
     mate = twin(zh, 1 - core)
     partners = (twin(zh + 1 - 2 * (zh % 2), core), twin(RING - 1 - zh, core))
-    norm_groups = (
-        [along(0, step) for step in (1, 2, 3)],
-        [along(1, step) for step in (1, 2, 3)] + [at(x, (y + step) % RING, 1 - z) for step in range(RING)],
-    )
+    norm_group = [
+        at((x + dx) % RING, (y + dy) % RING, (z + dz) % 2)
+        for dx, dy, dz in sorted(
+            itertools.product(range(RING), range(RING), range(2)),
+            key=lambda d: -min(d[0], RING - d[0]) - min(d[1], RING - d[1]) - d[2])
+        if (dx, dy, dz) != (0, 0, 0)
+    ]
 
     halves = cotangent.shape[1] // 2
 
@@ -130,7 +134,7 @@
         states[n].start()
 
     barrier = pltpu.get_barrier_semaphore()
-    everyone = norm_groups[0] + norm_groups[1] + [mate, *partners]
+    everyone = norm_group + [mate, *partners]
     for device in everyone:
         pl.semaphore_signal(barrier, inc=1, device_id=device, device_id_type=MESH)
     def copy_a(s, axis, i, way):
@@ -301,24 +305,18 @@
     for state in states:
         state.wait()
 
-    slot = 0
-    sent = []
-    for phase, group in enumerate(norm_groups):
-        norm_send[phase] = total
-        copies = [
-            pltpu.make_async_remote_copy(
-                src_ref=norm_send.at[phase], dst_ref=norm_recv.at[slot + n],
-                send_sem=ns_sem.at[slot + n], recv_sem=nr_sem.at[slot + n],
-                device_id=device, device_id_type=MESH)
-            for n, device in enumerate(group)
-        ]
-        for copy in copies:
-            copy.start()
-        for n, copy in enumerate(copies):
-            copy.wait_recv()
-            total = total + norm_recv[slot + n]
-        slot += len(group)
-        sent += copies
+    norm_send[...] = total
+    sent = [
+        pltpu.make_async_remote_copy(
+            src_ref=norm_send, dst_ref=norm_recv.at[n], send_sem=ns_sem.at[n], recv_sem=nr_sem.at[n],
+            device_id=device, device_id_type=MESH)
+        for n, device in enumerate(norm_group)
+    ]
+    for copy in sent:
+        copy.start()
+    for copy in sent:
+        copy.wait_recv()
+    total = total + jnp.sum(norm_recv[...], axis=0)
 
     mean_square = jnp.sum(total) / (hidden * cotangent.shape[1])
     clip_factor = jnp.minimum(1.0, lax.rsqrt(jnp.full((1, LANES), mean_square + clip_eps, jnp.float32)))
@@ -431,8 +429,8 @@
             *[vmem((count, 2, 2 * rows, LANES), bf16) for count, rows in zip(COUNTS, BLOCKS)] * 2,
             *[vmem((2 * rows, LANES), bf16) for rows in BLOCKS[:2]] * 2,
             *[vmem((ITEMS, 4 * BLOCKS[2], LANES), bf16)] * 2,
-            vmem((2, 8, LANES), f32),
-            vmem((10, 8, LANES), f32),
+            vmem((8, LANES), f32),
+            vmem((GROUP - 1, 8, LANES), f32),
             vmem((RING, piece, LANES), f32),
             vmem((RING, piece, LANES), f32),
             vmem((RING, 2, piece + PAD, LANES), bf16),
@@ -440,7 +438,7 @@
             vmem((2, RING, piece, LANES), f32),
             dma((2,)), dma((5,)),
             *[dma((3, count, 2))] * 4,
-            dma((2,)), dma((2,)), dma((ITEMS,)), dma((ITEMS,)), dma((10,)), dma((10,)), dma((RING,)), dma((RING,)),
+            dma((2,)), dma((2,)), dma((ITEMS,)), dma((ITEMS,)), dma((GROUP - 1,)), dma((GROUP - 1,)), dma((RING,)), dma((RING,)),
             dma((RING, 2)), dma((RING, 2)), dma((RING,)), dma((RING,)),
         ],
         compiler_params=pltpu.CompilerParams(

time: 72.2 us -> 70.4 us (0.975)
  Pallas kernels: 71.3 us -> 69.5 us
    pallas_call x1, Pallas kernels: 70 us -> 68.2 us  [shards(): pl.pallas_call(kernel, out_shape=(jax.ShapeDtypeStruct((hidden, columns),...]
where the time goes in v5:
time: 70.4 us; the launch traced here: 70.3 us
  Pallas kernels  69.5 us (99%)
  between operations  0.8 us (1%)
    pallas_call x1, Pallas kernels, shards(): pl.pallas_call(kernel, out_shape=(jax.ShapeDtypeStruct((hidden, columns),...  68.2 us

profile of v5, /device:TPU:1, one launch (start us, length us, event | category | flops | bytes accessed | tf_op | source)
XLA Modules:
  0.0 70.3 jit_solution(4330236483171873740)
XLA Ops:
  0.6 68.2 %shard_map.102 = (f32[448,256]{1,0:T(8,128)S(1)}, f32[448,256]{1,0:T(8,128)S(1)}, f32[448,256]{1,0:T(8,128)S(1)}, f32[448,256]{1,0:T(8,128)S(1)}) custom-call(bf16[512,8192]{1,0:T(8,128)(2,1)} %bitcast.9, bf16[448,512]{1,0:T(8,128)(2,1)} %bitcast.10, f32[448,256]{1,0:T(8,128)} %bitcast.11, f32[448,256]{1,0:T(8,128)} %bitcast.12, f32[448,256]{1,0:T(8,128)} %bitcast.13, ...), custom_call_target="tpu_custom_call" | custom-call | flops 3758096384 | bytes 12000000 | tf_op jit(solution)/shard_map/pallas_call | solution.py:418
  68.9 1.3 %shard_map.103 = (f32[448,256]{1,0:T(8,128)}, f32[448,256]{1,0:T(8,128)}, f32[448,256]{1,0:T(8,128)}, f32[448,256]{1,0:T(8,128)}) custom-call(f32[448,256]{1,0:T(8,128)S(1)} %get-tuple-element.12.refs_0_, f32[448,256]{1,0:T(8,128)S(1)} %get-tuple-element.13.refs_1_, f32[448,256]{1,0:T(8,128)S(1)} %get-tuple-element.14.refs_2_, ...), custom_call_target="tpu_custom_call" | custom-call | bytes 3670016 | tf_op jit(solution)/shard_map/pallas_call | solution.py:449
